TPU v7x, 32 devices: a whole 2x2x4 slice. The times are simulated.
32 devices in a mesh: band: 4 (over z), dom: 8 (over y, x, core).
Axes of the slice: x: 2, y: 2, z: 4, core: 2. Of those that a mesh axis runs over, the one named last changes fastest.
Arguments:
- orbitals: bfloat16 [32, 32, 24576], P('band', 'dom'), may hold values from -6 to 6
- occupations: int32 [32], P('band'), may hold values from 1 to 4
Outputs:
- potential: float32 [32, 24576], P('dom')
- applied: bfloat16 [32, 32, 24576], P('band', 'dom')
All inputs are finite; a program needn't handle non-finite values.
Results may differ from a plain program's by a relative error of at most 0.0029.
Values sent between devices are 32-bit elements; how exact they have to be, the bound alone decides.
A program may use at most 128 MiB of HBM per device.

v0:
```python
import functools

import jax
import jax.numpy as jnp
import numpy as np
from jax import lax
from jax.experimental import pallas as pl
from jax.experimental.pallas import tpu as pltpu
from jax.sharding import PartitionSpec as P

NX = 128
NY = 192
COARSE = 48

screening = 0.02
relaxation = 0.8
charge_scale = 0.07

PLANES = 4
HALO = 6
OWN = HALO
WINDOW = PLANES + 2 * HALO
PAD = 8
CHUNKS = 8
MOST = (4, 4, 8)
STEP = NY // CHUNKS
CENTRE = [6.0 + screening * 4.0**level for level in range(4)]
GAIN = [relaxation / centre for centre in CENTRE]
KEEP = 1.0 - relaxation


def sines(n):
    k = np.arange(1, n + 1)
    basis = np.sqrt(2.0 / (n + 1)) * np.sin(np.pi * np.outer(k, k) / (n + 1))
    return basis, 2.0 * np.cos(np.pi * k / (n + 1))


def coarse_basis(depth):
    rows, cols, copies = NY // 8, NX // 8, 8
    sz, ez = sines(depth)
    sy, ey = sines(rows)
    sx, ex = sines(cols)
    left = np.kron(sz, sy)
    into = np.zeros((NX, NX))
    into[::copies, :cols] = sx
    back = np.zeros((NX, NX))
    back[:cols] = np.repeat(sx, copies, axis=1)
    near = (ez[:, None] + ey[None, :]).reshape(-1, 1) + ex[None, :]
    rate = KEEP + GAIN[3] * near
    total = GAIN[3] * sum(rate**n for n in range(COARSE))
    weight = np.zeros((depth * rows, NX))
    weight[:, :cols] = total
    return [np.asarray(part, np.float32) for part in (left, into, back, weight)]


def kernel(
    bands, domains,
    rho, left, into, back, weight,
    out,
    acc, from_outer, from_inner, fx, va, vb, vc, hv, t0, t1, t2, t3, g,
    f1, u1a, u1b, f2, u2a, u2b, f3,
    up_s, up_r, mid_s, mid_r, down_s, down_r, near_s, near_r, far_s, far_r, hv_s, hv_r, g_s, g_r,
):
    b = lax.axis_index("band")
    d = lax.axis_index("dom")
    half = bands // 2
    lower = b < half
    inner = jnp.where(lower, b + 1, b - 1)
    outer = jnp.where(lower, b - 1, b + 1)
    has_outer = jnp.logical_and(b > 0, b < bands - 1)
    centre = jnp.logical_or(b == half - 1, b == half)
    n1, n2, n3 = 2 * domains, domains, domains // 2

    def remote(src, dst, ss, rs, dev):
        return pltpu.make_async_remote_copy(
            src_ref=src, dst_ref=dst, send_sem=ss, recv_sem=rs,
            device_id=dev, device_id_type=pl.DeviceIdType.MESH,
        )

    fx[...] = jnp.zeros_like(fx)
    barrier = pltpu.get_barrier_semaphore()

    def greet(dev):
        pl.semaphore_signal(barrier, inc=1, device_id=dev, device_id_type=pl.DeviceIdType.MESH)

    for i in range(1, domains):
        greet((b, lax.rem(d + i, domains)))
    greet((inner, d))

    @pl.when(has_outer)
    def _():
        greet((outer, d))

    for ref in (va, vb, vc, f1, u1a, u1b, f2, u2a, u2b):
        ref[...] = jnp.zeros_like(ref)

    pl.semaphore_wait(barrier, domains + jnp.where(has_outer, 1, 0))

    def part(ref, c):
        return ref.at[:, pl.ds(c * STEP, STEP), :]

    def slab(c):
        return fx.at[pl.ds(OWN, PLANES), pl.ds(PAD + c * STEP, STEP), :]

    def up(c):
        return remote(part(acc, c), part(from_outer, c), up_s.at[c], up_r.at[c], (inner, d))

    def mid(c):
        return remote(part(acc, c), part(from_inner, c), mid_s.at[c], mid_r.at[c], (inner, d))

    def down(c, dev):
        return remote(slab(c), slab(c), down_s.at[c], down_r.at[c], (dev, d))

    def near_up(c):
        rows = pl.ds(PAD + c * STEP, STEP)
        return remote(
            fx.at[pl.ds(OWN + 2, 2), rows, :], fx.at[pl.ds(OWN - 2, 2), rows, :],
            near_s.at[0, c], near_r.at[0, c], (b, d + 1),
        )

    def near_down(c):
        rows = pl.ds(PAD + c * STEP, STEP)
        return remote(
            fx.at[pl.ds(OWN, 2), rows, :], fx.at[pl.ds(OWN + 4, 2), rows, :],
            near_s.at[1, c], near_r.at[1, c], (b, d - 1),
        )

    def gathered(c, at_centre):
        rows = slice(c * STEP, (c + 1) * STEP)

        @pl.when(has_outer)
        def _():
            up(c).wait_recv()
            acc[:, rows, :] = rho[:, rows, :] + from_outer[:, rows, :]

        @pl.when(jnp.logical_not(has_outer))
        def _():
            acc[:, rows, :] = rho[:, rows, :]

        (mid(c) if at_centre else up(c)).start()

    def spread(c, at_centre):
        rows = slice(c * STEP, (c + 1) * STEP)
        if at_centre:
            mid(c).wait_recv()
            fx[OWN:OWN + PLANES, PAD + c * STEP:PAD + (c + 1) * STEP, :] = (
                acc[:, rows, :] + from_inner[:, rows, :]
            )
        else:
            down(c, inner).wait_recv()

        @pl.when(has_outer)
        def _():
            down(c, outer).start()

        @pl.when(d < domains - 1)
        def _():
            near_up(c).start()

        @pl.when(d > 0)
        def _():
            near_down(c).start()

    @pl.when(centre)
    def _():
        for c in range(CHUNKS):
            gathered(c, True)
            if c > 0:
                spread(c - 1, True)
        spread(CHUNKS - 1, True)

    @pl.when(jnp.logical_not(centre))
    def _():
        for c in range(CHUNKS):
            gathered(c, False)
        for c in range(CHUNKS):
            spread(c, False)

    for c in range(CHUNKS):
        @pl.when(d < domains - 1)
        def _():
            near_down(c).wait_recv()

        @pl.when(d > 0)
        def _():
            near_up(c).wait_recv()

    def beside(src, p, r0, rn, width):
        c = src[p, PAD + r0:PAD + r0 + rn, :]
        lane = lax.broadcasted_iota(jnp.int32, (rn, NX), 1)
        total = src[p, PAD + r0 - 1:PAD + r0 + rn - 1, :] + src[p, PAD + r0 + 1:PAD + r0 + rn + 1, :]
        total = total + (src[p - 1, PAD + r0:PAD + r0 + rn, :] + src[p + 1, PAD + r0:PAD + r0 + rn, :])
        total = total + jnp.where(lane < width, 0.0, pltpu.roll(c, width, 1))
        total = total + jnp.where(lane >= NX - width, 0.0, pltpu.roll(c, NX - width, 1))
        return c, total

    def rows_of(level):
        return NY >> level

    def blocks(level):
        rn = 48 if rows_of(level) % 48 == 0 else rows_of(level)
        return [(r0, rn) for r0 in range(0, rows_of(level), rn)]

    def loop(lo, count, fn, most=4):
        group = max(n for n in range(1, most + 1) if count % n == 0)

        def step(i, carry):
            for j in range(group):
                fn(lo + i * group + j, j)
            return carry

        lax.fori_loop(0, count // group, step, 0)

    def gain(level, p):
        if level:
            return GAIN[level]
        z = PLANES * d - OWN + p
        inside = jnp.logical_and(z >= 0, z < PLANES * domains)
        return jnp.where(inside, jnp.float32(GAIN[0]), jnp.float32(0.0))

    def first(src, dst, level, lo, count):
        def plane(p, j):
            k = gain(level, p)
            for r0, rn in blocks(level):
                c, total = beside(src, p, r0, rn, 1 << level)
                dst[p, PAD + r0:PAD + r0 + rn, :] = (GAIN[level] * (1.0 + KEEP)) * c + (k * GAIN[level]) * total

        loop(lo, count, plane, MOST[level])

    def sweep(src, source, dst, level, lo, count):
        def plane(p, j):
            k = gain(level, p)
            for r0, rn in blocks(level):
                c, total = beside(src, p, r0, rn, 1 << level)
                f = source[p, PAD + r0:PAD + r0 + rn, :]
                dst[p, PAD + r0:PAD + r0 + rn, :] = KEEP * c + k * (f + total)

        loop(lo, count, plane, MOST[level])

    def residual(v, source, level, p, r0, rn):
        c, total = beside(v, p, r0, rn, 1 << level)
        return source[p, PAD + r0:PAD + r0 + rn, :] + total - CENTRE[level] * c

    spare = (t0, t1, t2, t3)

    def pooled(v, source, level, p, t):
        for r0, rn in blocks(level):
            t[r0:r0 + rn, :] = residual(v, source, level, p, r0, rn) + residual(v, source, level, p + 1, r0, rn)
        n = rows_of(level) // 2
        return t[pl.ds(0, n, stride=2), :] + t[pl.ds(1, n, stride=2), :]

    def window(h):
        return OWN - h, PLANES + 2 * h

    rows1 = NY // 2
    even = lax.broadcasted_iota(jnp.int32, (rows1, NX), 1) % 2 == 0

    def give(cycle, i):
        return remote(
            g.at[cycle, d], g.at[cycle, d], g_s.at[cycle, i], g_r.at[cycle, i],
            (b, lax.rem(d + i, domains)),
        )

    def take(cycle, i):
        origin = lax.rem(d + (domains - i), domains)
        return origin, remote(
            g.at[cycle, origin], g.at[cycle, origin], g_s.at[cycle, i], g_r.at[cycle, i], (b, origin)
        )

    def restrict_and_send(v, cycle):
        a = pooled(v, fx, 0, OWN, t0)
        a = a + pltpu.roll(a, NX - 1, 1)
        e = pooled(v, fx, 0, OWN + 2, t1)
        e = e + pltpu.roll(e, 1, 1)
        g[cycle, d] = 0.5 * jnp.where(even, a, e)
        for i in range(1, domains):
            give(cycle, i).start()

    def unpack(cycle, origin):
        a = g[cycle, origin]
        f1[1 + 2 * origin, PAD:PAD + rows1, :] = jnp.where(even, a, pltpu.roll(a, 1, 1))
        f1[2 + 2 * origin, PAD:PAD + rows1, :] = jnp.where(even, pltpu.roll(a, NX - 1, 1), a)

    def widen(a, level):
        width = 1 << level
        lane = lax.broadcasted_iota(jnp.int32, a.shape, 1)
        low = (lane // width) % 2 == 0
        return 0.5 * (a + jnp.where(low, pltpu.roll(a, NX - width, 1), pltpu.roll(a, width, 1)))

    def add_rows(dst, p, value, n):
        for odd in range(2):
            at = (p, pl.ds(PAD + odd, n, stride=2), slice(None))
            dst[at] = dst[at] + value

    def coarse(cycle, near):
        unpack(cycle, d)
        for i in range(1, domains):
            origin, copy = take(cycle, i)
            copy.wait_recv()
            unpack(cycle, origin)
        first(f1, u1a, 1, 1, n1)

        def down1(q, j):
            f2[1 + q, PAD:PAD + NY // 4, :] = widen(pooled(u1a, f1, 1, 1 + 2 * q, spare[j]), 1)

        loop(0, n2, down1)
        first(f2, u2a, 2, 1, n2)
        rows3 = NY // 8

        def down2(q, j):
            f3[pl.ds(pl.multiple_of(q * rows3, 8), rows3), :] = widen(pooled(u2a, f2, 2, 1 + 2 * q, spare[j]), 2)

        loop(0, n3, down2)
        dot = functools.partial(
            jnp.dot, precision=lax.Precision.HIGHEST, preferred_element_type=jnp.float32
        )
        modes = dot(left[...], dot(f3[...], into[...])) * weight[...]
        f3[...] = dot(dot(left[...], modes), back[...])

        def back2(q, j):
            value = f3[pl.ds(pl.multiple_of(q * rows3, 8), rows3), :]
            add_rows(u2a, 1 + 2 * q, value, rows3)
            add_rows(u2a, 2 + 2 * q, value, rows3)

        loop(0, n3, back2)
        sweep(u2a, f2, u2b, 2, 1, n2)
        sweep(u2b, f2, u2a, 2, 1, n2)

        def back1(q, j):
            value = u2a[1 + q, PAD:PAD + NY // 4, :]
            add_rows(u1a, 1 + 2 * q, value, NY // 4)
            add_rows(u1a, 2 + 2 * q, value, NY // 4)

        loop(0, n2, back1)
        for extra, src, dst in ((1, u1a, u1b), (0, u1b, u1a)):
            count = min(n1, 2 + 2 * (near + extra))
            start = jnp.clip(2 * d - near - extra, 0, n1 - count)
            sweep(src, f1, dst, 1, start + 1, count)

    def correct(v, near):
        for j in range(-near, 2 + near):
            z = 2 * d + j
            w = 2 * j + OWN

            @pl.when(jnp.logical_and(z >= 0, z < n1))
            def _():
                value = u1a[z + 1, PAD:PAD + rows1, :]
                add_rows(v, w, value, rows1)
                add_rows(v, w + 1, value, rows1)

    far = [
        (OWN, OWN - 4, 1, d < domains - 1, d > 0),
        (OWN + 2, OWN + 6, -1, d > 0, d < domains - 1),
        (OWN + 2, OWN - 6, 2, d < domains - 2, d > 1),
        (OWN, OWN + 8, -2, d > 1, d < domains - 2),
    ]

    def far_copy(i):
        at, to, offset, _, _ = far[i]
        return remote(
            fx.at[pl.ds(at, 2), pl.ds(PAD, NY), :], fx.at[pl.ds(to, 2), pl.ds(PAD, NY), :],
            far_s.at[i], far_r.at[i], (b, d + offset),
        )

    for i in range(2):
        @pl.when(far[i][3])
        def _():
            far_copy(i).start()

    first(fx, vb, 0, *window(1))
    restrict_and_send(vb, 0)
    for i in range(2, 4):
        @pl.when(far[i][3])
        def _():
            far_copy(i).start()

    coarse(0, 3)

    for i in range(4):
        @pl.when(far[i][4])
        def _():
            far_copy(i).wait_recv()

    first(fx, vb, 0, OWN - 5, 4)
    first(fx, vb, 0, OWN + PLANES + 1, 4)
    correct(vb, 3)
    sweep(vb, fx, va, 0, *window(4))
    sweep(va, fx, vb, 0, *window(3))

    sweep(vb, fx, va, 0, *window(2))
    sweep(va, fx, vc, 0, *window(1))
    restrict_and_send(vc, 1)

    def v_up():
        return remote(
            vc.at[pl.ds(OWN + 2, 2), pl.ds(PAD, NY), :], hv.at[0], hv_s.at[0], hv_r.at[0], (b, d + 1)
        )

    def v_down():
        return remote(
            vc.at[pl.ds(OWN, 2), pl.ds(PAD, NY), :], hv.at[1], hv_s.at[1], hv_r.at[1], (b, d - 1)
        )

    @pl.when(d < domains - 1)
    def _():
        v_up().start()

    @pl.when(d > 0)
    def _():
        v_down().start()

    coarse(1, 1)

    @pl.when(d < domains - 1)
    def _():
        v_up().wait_send()
        v_down().wait_recv()
        vc[OWN + 4:OWN + 6, PAD:PAD + NY, :] = hv[1]

    @pl.when(d > 0)
    def _():
        v_down().wait_send()
        v_up().wait_recv()
        vc[OWN - 2:OWN, PAD:PAD + NY, :] = hv[0]

    correct(vc, 1)
    sweep(vc, fx, va, 0, *window(1))
    for p in range(PLANES):
        for r0, rn in blocks(0):
            c, total = beside(va, OWN + p, r0, rn, 1)
            f = fx[OWN + p, PAD + r0:PAD + r0 + rn, :]
            out[p, r0:r0 + rn, :] = KEEP * c + GAIN[0] * (f + total)

    for c in range(CHUNKS):
        @pl.when(centre)
        def _():
            mid(c).wait_send()

        @pl.when(jnp.logical_not(centre))
        def _():
            up(c).wait_send()

        @pl.when(has_outer)
        def _():
            down(c, outer).wait_send()

        @pl.when(d < domains - 1)
        def _():
            near_up(c).wait_send()

        @pl.when(d > 0)
        def _():
            near_down(c).wait_send()

    for i in range(4):
        @pl.when(far[i][3])
        def _():
            far_copy(i).wait_send()

    for cycle in range(2):
        for i in range(1, domains):
            give(cycle, i).wait_send()


def potential_of(rho, bands, domains):
    n1, n2, n3 = 2 * domains, domains, domains // 2
    tables = coarse_basis(n3)
    f32 = jnp.float32
    slab = pltpu.VMEM((PLANES, NY, NX), f32)
    fine = pltpu.VMEM((WINDOW, NY + 2 * PAD, NX), f32)
    level1 = pltpu.VMEM((n1 + 2, NY // 2 + 2 * PAD, NX), f32)
    level2 = pltpu.VMEM((n2 + 2, NY // 4 + 2 * PAD, NX), f32)
    chunk_sems = pltpu.SemaphoreType.DMA((CHUNKS,))
    near_sems = pltpu.SemaphoreType.DMA((2, CHUNKS))
    gather_sems = pltpu.SemaphoreType.DMA((2, domains))
    vmem = pl.BlockSpec(memory_space=pltpu.VMEM)
    return pl.pallas_call(
        functools.partial(kernel, bands, domains),
        out_shape=jax.ShapeDtypeStruct((PLANES, NY, NX), f32),
        in_specs=[vmem] * 5,
        out_specs=vmem,
        scratch_shapes=[
            slab, slab, slab, fine, fine, fine, fine,
            pltpu.VMEM((2, 2, NY, NX), f32),
            *[pltpu.VMEM((NY, NX), f32)] * 4,
            pltpu.VMEM((2, domains, NY // 2, NX), f32),
            level1, level1, level1, level2, level2, level2,
            pltpu.VMEM((n3 * (NY // 8), NX), f32),
            chunk_sems, chunk_sems, chunk_sems, chunk_sems, chunk_sems, chunk_sems,
            near_sems, near_sems,
            pltpu.SemaphoreType.DMA((4,)), pltpu.SemaphoreType.DMA((4,)),
            pltpu.SemaphoreType.DMA((2,)), pltpu.SemaphoreType.DMA((2,)),
            gather_sems, gather_sems,
        ],
        compiler_params=pltpu.CompilerParams(
            collective_id=0, has_side_effects=True, vmem_limit_bytes=48 * 1024 * 1024
        ),
    )(rho, *[jnp.asarray(table) for table in tables])


def body(bands, domains, orbitals, occupations):
    planes = orbitals.shape[1]
    orbital_total = orbitals.shape[0] * bands
    weights = occupations.astype(jnp.float32) * (0.5 * charge_scale / orbital_total)
    values = orbitals.astype(jnp.float32)
    rho = jnp.sum(weights[:, None, None] * (values * values), axis=0)
    potential = potential_of(rho.reshape(planes, NY, NX), bands, domains)
    potential = potential.reshape(planes, NY * NX)
    applied = (potential[None] * values).astype(jnp.bfloat16)
    return (potential, applied)


def solution(mesh):
    return jax.shard_map(
        functools.partial(body, mesh.shape["band"], mesh.shape["dom"]),
        mesh=mesh,
        in_specs=(P("band", "dom", None), P("band")),
        out_specs=(P("dom", None), P("band", "dom", None)),
        check_vma=False,
    )
```

profile of v0, /device:TPU:1, one launch (start us, length us, event | category | flops | bytes accessed | tf_op | source)
XLA Modules:
  0.0 66.4 jit_solution(15464585399163894024)
XLA Ops:
  0.6 0.0 copy-start.2
  0.6 0.0 copy-start
  0.7 0.0 copy-start.1
  0.7 0.0 copy-start.3
  0.7 0.7 %convert_multiply_fusion.2 = f32[8]{0:T(128)S(1)} fusion(s32[8]{0:T(128)} %param.7), kind=kLoop, calls=%fused_computation.7 | loop fusion | flops 16 | bytes 64 | tf_op jit(solution)/shard_map/mul | solution.py:504
  1.4 2.6 %fusion.1 = f32[4,24576]{1,0:T(4,128)S(1)} fusion(bf16[8,4,24576]{2,1,0:T(4,128)(2,1)} %param.6, f32[8]{0:T(128)S(1)} %convert_multiply_fusion.2), kind=kLoop, calls=%fused_computation.3 | loop fusion | flops 3047424 | bytes 1966112 | tf_op jit(solution)/shard_map/reduce_sum | solution.py:506
  4.0 0.0 copy-start.4
  4.0 0.0 copy-done.2
  4.1 0.0 copy-done
  4.1 0.0 copy-done.1
  4.1 0.0 copy-done.3
  4.1 60.2 %shard_map.77 = f32[4,192,128]{2,1,0:T(8,128)S(1)} custom-call(f32[4,192,128]{2,1,0:T(8,128)S(1)} %bitcast.8, f32[96,96]{1,0:T(8,128)S(1)} %copy-done.3, f32[128,128]{1,0:T(8,128)S(1)} %copy-done.1, f32[128,128]{1,0:T(8,128)S(1)} %copy-done, f32[96,128]{1,0:T(8,128)S(1)} %copy-done.2), custom_call_target="tpu_custom_call" | custom-call | tf_op jit(solution)/shard_map/pallas_call | solution.py:477
  64.3 0.3 copy.12
  64.5 0.0 copy-start.5
  64.5 0.0 copy-done.4
  64.5 1.9 %fusion.2 = bf16[8,4,24576]{2,1,0:T(4,128)(2,1)} fusion(bf16[8,4,24576]{2,1,0:T(4,128)(2,1)S(1)} %copy-done.4, f32[4,24576]{1,0:T(4,128)S(1)} %bitcast.10), kind=kLoop, calls=%fused_computation.4 | loop fusion | flops 2359296 | bytes 3538944 | tf_op jit(solution)/shard_map/convert_element_type | solution.py:509
  66.4 0.0 copy-done.5
  (1 shorter events, 0.0 us)
Async XLA Ops:
  0.6 3.4 %copy-start.2 = (f32[96,128]{1,0:T(8,128)S(1)}, f32[96,128]{1,0:T(8,128)}, u32[]{:S(2)}) copy-start(f32[96,128]{1,0:T(8,128)} %constant.15.clone.weight) | copy-start | bytes 147460
  0.6 3.4 %copy-start = (f32[128,128]{1,0:T(8,128)S(1)}, f32[128,128]{1,0:T(8,128)}, u32[]{:S(2)}) copy-start(f32[128,128]{1,0:T(8,128)} %constant.14.clone.back) | copy-start | bytes 196612
  0.7 3.4 %copy-start.1 = (f32[128,128]{1,0:T(8,128)S(1)}, f32[128,128]{1,0:T(8,128)}, u32[]{:S(2)}) copy-start(f32[128,128]{1,0:T(8,128)} %constant.13.clone.into) | copy-start | bytes 196612
  0.7 3.4 %copy-start.3 = (f32[96,96]{1,0:T(8,128)S(1)}, f32[96,96]{1,0:T(8,128)}, u32[]{:S(2)}) copy-start(f32[96,96]{1,0:T(8,128)} %constant.12.clone.left) | copy-start | bytes 110596
  4.0 60.5 %copy-start.4 = (bf16[8,4,24576]{2,1,0:T(4,128)(2,1)S(1)}, bf16[8,4,24576]{2,1,0:T(4,128)(2,1)}, u32[]{:S(2)}) copy-start(bf16[8,4,24576]{2,1,0:T(4,128)(2,1)} %param.6) | copy-start | bytes 4718596
  64.5 1.9 %copy-start.5 = (f32[1,4,192,128]{3,1,2,0:T(4,128)}, f32[1,4,192,128]{3,1,2,0:T(4,128)S(1)}, u32[]{:S(2)}) copy-start(f32[1,4,192,128]{3,1,2,0:T(4,128)S(1)} %copy.12) | copy-start | bytes 1179652
where the time goes:
time: 66.6 us; the launch traced here: 66.4 us
  Pallas kernels  60.2 us (90%)
  other arithmetic  5.17 us (8%)
  between operations  0.74 us (1%)
    pallas_call x1, Pallas kernels, potential_of(): pl.pallas_call(functools.partial(kernel, bands, domains), out_shape=jax.S...  60.2 us
    reduce_sum x1, other arithmetic, body(): rho = jnp.sum(weights[:, None, None] * (values * values), axis=0)  2.6 us
    convert_element_type x1, other arithmetic, body(): applied = (potential[None] * values).astype(jnp.bfloat16)  1.85 us

commit v1 on v0

--- a/solution.py
+++ b/solution.py
@@ -22,8 +22,11 @@
 WINDOW = PLANES + 2 * HALO
 PAD = 8
 CHUNKS = 8
+LAG = 3
+HALVES = 2
 MOST = (4, 4, 8)
 STEP = NY // CHUNKS
+HALF = NY // HALVES
 CENTRE = [6.0 + screening * 4.0**level for level in range(4)]
 GAIN = [relaxation / centre for centre in CENTRE]
 KEEP = 1.0 - relaxation
@@ -125,6 +128,36 @@
             near_s.at[1, c], near_r.at[1, c], (b, d - 1),
         )
 
+    even_d = lax.rem(d, 2) == 0
+    odd_d = lax.rem(d, 2) == 1
+    far = [
+        (OWN, OWN - 4, 1, d < domains - 1, d > 0),
+        (OWN + 2, OWN + 6, -1, d > 0, d < domains - 1),
+        (OWN + 2, OWN - 6, 2, jnp.logical_and(even_d, d < domains - 2), d > 1),
+        (OWN, OWN + 8, -2, jnp.logical_and(odd_d, d > 1), d < domains - 2),
+    ]
+
+    def far_copy(i, h):
+        at, to, offset, _, _ = far[i]
+        rows = pl.ds(PAD + h * HALF, HALF)
+        return remote(
+            fx.at[pl.ds(at, 2), rows, :], fx.at[pl.ds(to, 2), rows, :],
+            far_s.at[i, h], far_r.at[i, h], (b, d + offset),
+        )
+
+    onward = [
+        (OWN - 2, OWN - 6, 1, 2, jnp.logical_and(even_d, d > 1)),
+        (OWN + 4, OWN + 8, -1, 3, jnp.logical_and(odd_d, d < domains - 2)),
+    ]
+
+    def onward_copy(i, h):
+        at, to, offset, slot, _ = onward[i]
+        rows = pl.ds(PAD + h * HALF, HALF)
+        return remote(
+            fx.at[pl.ds(at, 2), rows, :], fx.at[pl.ds(to, 2), rows, :],
+            far_s.at[slot + 2, h], far_r.at[slot, h], (b, d + offset),
+        )
+
     def gathered(c, at_centre):
         rows = slice(c * STEP, (c + 1) * STEP)
 
@@ -161,13 +194,19 @@
         def _():
             near_down(c).start()
 
+        if (c + 1) % (CHUNKS // HALVES) == 0:
+            for i in range(4):
+                @pl.when(far[i][3])
+                def _():
+                    far_copy(i, c // (CHUNKS // HALVES)).start()
+
     @pl.when(centre)
     def _():
-        for c in range(CHUNKS):
-            gathered(c, True)
-            if c > 0:
-                spread(c - 1, True)
-        spread(CHUNKS - 1, True)
+        for c in range(CHUNKS + LAG):
+            if c < CHUNKS:
+                gathered(c, True)
+            if c >= LAG:
+                spread(c - LAG, True)
 
     @pl.when(jnp.logical_not(centre))
     def _():
@@ -348,38 +387,21 @@
                 add_rows(v, w, value, rows1)
                 add_rows(v, w + 1, value, rows1)
 
-    far = [
-        (OWN, OWN - 4, 1, d < domains - 1, d > 0),
-        (OWN + 2, OWN + 6, -1, d > 0, d < domains - 1),
-        (OWN + 2, OWN - 6, 2, d < domains - 2, d > 1),
-        (OWN, OWN + 8, -2, d > 1, d < domains - 2),
-    ]
-
-    def far_copy(i):
-        at, to, offset, _, _ = far[i]
-        return remote(
-            fx.at[pl.ds(at, 2), pl.ds(PAD, NY), :], fx.at[pl.ds(to, 2), pl.ds(PAD, NY), :],
-            far_s.at[i], far_r.at[i], (b, d + offset),
-        )
-
     for i in range(2):
-        @pl.when(far[i][3])
-        def _():
-            far_copy(i).start()
+        @pl.when(onward[i][4])
+        def _():
+            for h in range(HALVES):
+                onward_copy(i, h).start()
 
     first(fx, vb, 0, *window(1))
     restrict_and_send(vb, 0)
-    for i in range(2, 4):
-        @pl.when(far[i][3])
-        def _():
-            far_copy(i).start()
-
     coarse(0, 3)
 
     for i in range(4):
         @pl.when(far[i][4])
         def _():
-            far_copy(i).wait_recv()
+            for h in range(HALVES):
+                far_copy(i, h).wait_recv()
 
     first(fx, vb, 0, OWN - 5, 4)
     first(fx, vb, 0, OWN + PLANES + 1, 4)
@@ -455,7 +477,14 @@
     for i in range(4):
         @pl.when(far[i][3])
         def _():
-            far_copy(i).wait_send()
+            for h in range(HALVES):
+                far_copy(i, h).wait_send()
+
+    for i in range(2):
+        @pl.when(onward[i][4])
+        def _():
+            for h in range(HALVES):
+                onward_copy(i, h).wait_send()
 
     for cycle in range(2):
         for i in range(1, domains):
@@ -488,7 +517,7 @@
             pltpu.VMEM((n3 * (NY // 8), NX), f32),
             chunk_sems, chunk_sems, chunk_sems, chunk_sems, chunk_sems, chunk_sems,
             near_sems, near_sems,
-            pltpu.SemaphoreType.DMA((4,)), pltpu.SemaphoreType.DMA((4,)),
+            pltpu.SemaphoreType.DMA((6, HALVES)), pltpu.SemaphoreType.DMA((4, HALVES)),
             pltpu.SemaphoreType.DMA((2,)), pltpu.SemaphoreType.DMA((2,)),
             gather_sems, gather_sems,
         ],

time: 66.6 us -> 60.9 us (0.914)
  Pallas kernels: 60.2 us -> 54.5 us
    pallas_call x1, Pallas kernels: 60.2 us -> 54.5 us  [potential_of(): pl.pallas_call(functools.partial(kernel, bands, domains), out_shape=jax.S...]
where the time goes in v1:
time: 60.9 us; the launch traced here: 60.8 us
  Pallas kernels  54.5 us (89%)
  other arithmetic  5.17 us (8%)
  between operations  0.74 us (1%)
    pallas_call x1, Pallas kernels, potential_of(): pl.pallas_call(functools.partial(kernel, bands, domains), out_shape=jax.S...  54.5 us
    reduce_sum x1, other arithmetic, body(): rho = jnp.sum(weights[:, None, None] * (values * values), axis=0)  2.6 us
    convert_element_type x1, other arithmetic, body(): applied = (potential[None] * values).astype(jnp.bfloat16)  1.85 us

profile of v1, /device:TPU:1, one launch (start us, length us, event | category | flops | bytes accessed | tf_op | source)
XLA Modules:
  0.0 60.8 jit_solution(13225247866699516448)
XLA Ops:
  0.6 0.0 copy-start.2
  0.6 0.0 copy-start
  0.7 0.0 copy-start.1
  0.7 0.0 copy-start.3
  0.7 0.7 %convert_multiply_fusion.2 = f32[8]{0:T(128)S(1)} fusion(s32[8]{0:T(128)} %param.7), kind=kLoop, calls=%fused_computation.7 | loop fusion | flops 16 | bytes 64 | tf_op jit(solution)/shard_map/mul | solution.py:533
  1.4 2.6 %fusion.1 = f32[4,24576]{1,0:T(4,128)S(1)} fusion(bf16[8,4,24576]{2,1,0:T(4,128)(2,1)} %param.6, f32[8]{0:T(128)S(1)} %convert_multiply_fusion.2), kind=kLoop, calls=%fused_computation.3 | loop fusion | flops 3047424 | bytes 1966112 | tf_op jit(solution)/shard_map/reduce_sum | solution.py:535
  4.0 0.0 copy-start.4
  4.0 0.0 copy-done.2
  4.1 0.0 copy-done
  4.1 0.0 copy-done.1
  4.1 0.0 copy-done.3
  4.1 54.5 %shard_map.77 = f32[4,192,128]{2,1,0:T(8,128)S(1)} custom-call(f32[4,192,128]{2,1,0:T(8,128)S(1)} %bitcast.8, f32[96,96]{1,0:T(8,128)S(1)} %copy-done.3, f32[128,128]{1,0:T(8,128)S(1)} %copy-done.1, f32[128,128]{1,0:T(8,128)S(1)} %copy-done, f32[96,128]{1,0:T(8,128)S(1)} %copy-done.2), custom_call_target="tpu_custom_call" | custom-call | tf_op jit(solution)/shard_map/pallas_call | solution.py:506
  58.6 0.3 copy.12
  58.9 0.0 copy-start.5
  58.9 0.0 copy-done.4
  58.9 1.9 %fusion.2 = bf16[8,4,24576]{2,1,0:T(4,128)(2,1)} fusion(bf16[8,4,24576]{2,1,0:T(4,128)(2,1)S(1)} %copy-done.4, f32[4,24576]{1,0:T(4,128)S(1)} %bitcast.10), kind=kLoop, calls=%fused_computation.4 | loop fusion | flops 2359296 | bytes 3538944 | tf_op jit(solution)/shard_map/convert_element_type | solution.py:538
  60.8 0.0 copy-done.5
  (1 shorter events, 0.0 us)
Async XLA Ops:
  0.6 3.4 %copy-start.2 = (f32[96,128]{1,0:T(8,128)S(1)}, f32[96,128]{1,0:T(8,128)}, u32[]{:S(2)}) copy-start(f32[96,128]{1,0:T(8,128)} %constant.15.clone.weight) | copy-start | bytes 147460
  0.6 3.4 %copy-start = (f32[128,128]{1,0:T(8,128)S(1)}, f32[128,128]{1,0:T(8,128)}, u32[]{:S(2)}) copy-start(f32[128,128]{1,0:T(8,128)} %constant.14.clone.back) | copy-start | bytes 196612
  0.7 3.4 %copy-start.1 = (f32[128,128]{1,0:T(8,128)S(1)}, f32[128,128]{1,0:T(8,128)}, u32[]{:S(2)}) copy-start(f32[128,128]{1,0:T(8,128)} %constant.13.clone.into) | copy-start | bytes 196612
  0.7 3.4 %copy-start.3 = (f32[96,96]{1,0:T(8,128)S(1)}, f32[96,96]{1,0:T(8,128)}, u32[]{:S(2)}) copy-start(f32[96,96]{1,0:T(8,128)} %constant.12.clone.left) | copy-start | bytes 110596
  4.0 54.9 %copy-start.4 = (bf16[8,4,24576]{2,1,0:T(4,128)(2,1)S(1)}, bf16[8,4,24576]{2,1,0:T(4,128)(2,1)}, u32[]{:S(2)}) copy-start(bf16[8,4,24576]{2,1,0:T(4,128)(2,1)} %param.6) | copy-start | bytes 4718596
  58.9 1.9 %copy-start.5 = (f32[1,4,192,128]{3,1,2,0:T(4,128)}, f32[1,4,192,128]{3,1,2,0:T(4,128)S(1)}, u32[]{:S(2)}) copy-start(f32[1,4,192,128]{3,1,2,0:T(4,128)S(1)} %copy.12) | copy-start | bytes 1179652

commit v2 on v1

--- a/solution.py
+++ b/solution.py
@@ -23,6 +23,7 @@
 PAD = 8
 CHUNKS = 8
 LAG = 3
+AHEAD = 2
 HALVES = 2
 MOST = (4, 4, 8)
 STEP = NY // CHUNKS
@@ -57,9 +58,10 @@
 
 
 def kernel(
-    bands, domains,
-    rho, left, into, back, weight,
+    bands, domains, scale,
+    occupations, orbitals, left_in, into_in, back_in, weight_in,
     out,
+    occ, left, into, back, weight, held, mixed, out_s, table_s, held_s,
     acc, from_outer, from_inner, fx, va, vb, vc, hv, t0, t1, t2, t3, g,
     f1, u1a, u1b, f2, u2a, u2b, f3,
     up_s, up_r, mid_s, mid_r, down_s, down_r, near_s, near_r, far_s, far_r, hv_s, hv_r, g_s, g_r,
@@ -80,7 +82,26 @@
             device_id=dev, device_id_type=pl.DeviceIdType.MESH,
         )
 
-    fx[...] = jnp.zeros_like(fx)
+    lanes = STEP * NX
+
+    def fetch(c):
+        at = (slice(None), slice(None), pl.ds(c * lanes, lanes))
+        return pltpu.make_async_copy(orbitals.at[at], held.at[at], held_s.at[c])
+
+    def result(p):
+        return pltpu.make_async_copy(acc.at[p], out.at[p], out_s.at[p])
+
+    tables = [
+        pltpu.make_async_copy(src, dst, table_s.at[i])
+        for i, (src, dst) in enumerate(
+            ((occupations, occ), (left_in, left), (into_in, into), (back_in, back), (weight_in, weight))
+        )
+    ]
+    tables[0].start()
+    for c in range(CHUNKS):
+        fetch(c).start()
+    for table in tables[1:]:
+        table.start()
     barrier = pltpu.get_barrier_semaphore()
 
     def greet(dev):
@@ -94,9 +115,47 @@
     def _():
         greet((outer, d))
 
-    for ref in (va, vb, vc, f1, u1a, u1b, f2, u2a, u2b):
-        ref[...] = jnp.zeros_like(ref)
-
+    for ref in (fx, va, vb, vc, f1, u1a, u1b, f2, u2a, u2b):
+        edge = jnp.zeros((ref.shape[0], PAD, NX), jnp.float32)
+        ref[:, 0:PAD, :] = edge
+        ref[:, ref.shape[1] - PAD:ref.shape[1], :] = edge
+
+    def clear(ref, p):
+        ref[p] = jnp.zeros(ref.shape[1:], jnp.float32)
+
+    for ref in (f1, u1a, u1b, f2, u2a, u2b):
+        clear(ref, 0)
+        clear(ref, ref.shape[0] - 1)
+    clear(vc, OWN - 2)
+    clear(vc, OWN + 5)
+    for k in range(HALO):
+        reach = -(-(HALO - k) // PLANES)
+
+        @pl.when(d < reach)
+        def _():
+            clear(fx, k)
+
+        @pl.when(d >= domains - reach)
+        def _():
+            clear(fx, WINDOW - 1 - k)
+
+    def density(c):
+        fetch(c).wait()
+        total = None
+        for i in range(orbitals.shape[0]):
+            value = held[i, :, c * lanes:(c + 1) * lanes].astype(jnp.float32)
+            term = (occ[i].astype(jnp.float32) * scale) * (value * value)
+            total = term if total is None else total + term
+        first_row = c * STEP * PLANES
+        for y in range(STEP):
+            at = first_row + y * PLANES
+            mixed[at:at + PLANES, :] = total[:, y * NX:(y + 1) * NX]
+        for p in range(PLANES):
+            acc[p, c * STEP:(c + 1) * STEP, :] = mixed[pl.ds(first_row + p, STEP, stride=PLANES), :]
+
+    tables[0].wait()
+    for c in range(AHEAD):
+        density(c)
     pl.semaphore_wait(barrier, domains + jnp.where(has_outer, 1, 0))
 
     def part(ref, c):
@@ -161,14 +220,13 @@
     def gathered(c, at_centre):
         rows = slice(c * STEP, (c + 1) * STEP)
 
+        if c >= AHEAD:
+            density(c)
+
         @pl.when(has_outer)
         def _():
             up(c).wait_recv()
-            acc[:, rows, :] = rho[:, rows, :] + from_outer[:, rows, :]
-
-        @pl.when(jnp.logical_not(has_outer))
-        def _():
-            acc[:, rows, :] = rho[:, rows, :]
+            acc[:, rows, :] = acc[:, rows, :] + from_outer[:, rows, :]
 
         (mid(c) if at_centre else up(c)).start()
 
@@ -395,6 +453,8 @@
 
     first(fx, vb, 0, *window(1))
     restrict_and_send(vb, 0)
+    for table in tables[1:]:
+        table.wait()
     coarse(0, 3)
 
     for i in range(4):
@@ -444,6 +504,15 @@
         v_down().wait_send()
         v_up().wait_recv()
         vc[OWN - 2:OWN, PAD:PAD + NY, :] = hv[0]
+
+    for c in range(CHUNKS):
+        @pl.when(centre)
+        def _():
+            mid(c).wait_send()
+
+        @pl.when(jnp.logical_not(centre))
+        def _():
+            up(c).wait_send()
 
     correct(vc, 1)
     sweep(vc, fx, va, 0, *window(1))
@@ -451,17 +520,12 @@
         for r0, rn in blocks(0):
             c, total = beside(va, OWN + p, r0, rn, 1)
             f = fx[OWN + p, PAD + r0:PAD + r0 + rn, :]
-            out[p, r0:r0 + rn, :] = KEEP * c + GAIN[0] * (f + total)
+            acc[p, r0:r0 + rn, :] = KEEP * c + GAIN[0] * (f + total)
+        result(p).start()
+    for p in range(PLANES):
+        result(p).wait()
 
     for c in range(CHUNKS):
-        @pl.when(centre)
-        def _():
-            mid(c).wait_send()
-
-        @pl.when(jnp.logical_not(centre))
-        def _():
-            up(c).wait_send()
-
         @pl.when(has_outer)
         def _():
             down(c, outer).wait_send()
@@ -491,10 +555,11 @@
             give(cycle, i).wait_send()
 
 
-def potential_of(rho, bands, domains):
+def potential_of(orbitals, occupations, bands, domains):
     n1, n2, n3 = 2 * domains, domains, domains // 2
     tables = coarse_basis(n3)
     f32 = jnp.float32
+    count = orbitals.shape[0]
     slab = pltpu.VMEM((PLANES, NY, NX), f32)
     fine = pltpu.VMEM((WINDOW, NY + 2 * PAD, NX), f32)
     level1 = pltpu.VMEM((n1 + 2, NY // 2 + 2 * PAD, NX), f32)
@@ -502,13 +567,17 @@
     chunk_sems = pltpu.SemaphoreType.DMA((CHUNKS,))
     near_sems = pltpu.SemaphoreType.DMA((2, CHUNKS))
     gather_sems = pltpu.SemaphoreType.DMA((2, domains))
-    vmem = pl.BlockSpec(memory_space=pltpu.VMEM)
     return pl.pallas_call(
-        functools.partial(kernel, bands, domains),
+        functools.partial(kernel, bands, domains, 0.5 * charge_scale / (count * bands)),
         out_shape=jax.ShapeDtypeStruct((PLANES, NY, NX), f32),
-        in_specs=[vmem] * 5,
-        out_specs=vmem,
+        in_specs=[pl.BlockSpec(memory_space=pl.ANY)] * 6,
+        out_specs=pl.BlockSpec(memory_space=pl.ANY),
         scratch_shapes=[
+            pltpu.SMEM(occupations.shape, jnp.int32),
+            *[pltpu.VMEM(table.shape, f32) for table in tables],
+            pltpu.VMEM(orbitals.shape, orbitals.dtype),
+            pltpu.VMEM((NY * PLANES, NX), f32),
+            pltpu.SemaphoreType.DMA((PLANES,)), pltpu.SemaphoreType.DMA((5,)), chunk_sems,
             slab, slab, slab, fine, fine, fine, fine,
             pltpu.VMEM((2, 2, NY, NX), f32),
             *[pltpu.VMEM((NY, NX), f32)] * 4,
@@ -522,19 +591,14 @@
             gather_sems, gather_sems,
         ],
         compiler_params=pltpu.CompilerParams(
-            collective_id=0, has_side_effects=True, vmem_limit_bytes=48 * 1024 * 1024
+            collective_id=0, has_side_effects=True, vmem_limit_bytes=62_500_000
         ),
-    )(rho, *[jnp.asarray(table) for table in tables])
+    )(occupations, orbitals, *[jnp.asarray(table) for table in tables])
 
 
 def body(bands, domains, orbitals, occupations):
-    planes = orbitals.shape[1]
-    orbital_total = orbitals.shape[0] * bands
-    weights = occupations.astype(jnp.float32) * (0.5 * charge_scale / orbital_total)
     values = orbitals.astype(jnp.float32)
-    rho = jnp.sum(weights[:, None, None] * (values * values), axis=0)
-    potential = potential_of(rho.reshape(planes, NY, NX), bands, domains)
-    potential = potential.reshape(planes, NY * NX)
+    potential = potential_of(orbitals, occupations, bands, domains).reshape(orbitals.shape[1], NY * NX)
     applied = (potential[None] * values).astype(jnp.bfloat16)
     return (potential, applied)
 

time: 60.9 us -> 59.2 us (0.972)
  other arithmetic: 5.17 us -> 1.87 us
  local copies, waits for them, and re-layouts: 0.32 us -> 1.26 us
  Pallas kernels: 54.5 us -> 55.2 us
    reduce_sum x1 -> x0, other arithmetic: 2.6 us -> none  [body(): rho = jnp.sum(weights[:, None, None] * (values * values), axis=0)]
    unnamed x14 -> x5, local copies, waits for them, and re-layouts: 0.32 us -> 1.26 us
    mul x1 -> x0, other arithmetic: 0.72 us -> none  [body(): occupations.astype(jnp.float32) * (0.5 * charge_scale / orbital_total)]
    pallas_call x1, Pallas kernels: 54.5 us -> 55.2 us  [potential_of(): pl.pallas_call(functools.partial(kernel, bands, domains, 0.5 * charge_sca...]
where the time goes in v2:
time: 59.2 us; the launch traced here: 59 us
  Pallas kernels  55.2 us (93%)
  other arithmetic  1.87 us (3%)
  local copies, waits for them, and re-layouts  1.26 us (2%)
  between operations  0.66 us (1%)
    pallas_call x1, Pallas kernels, potential_of(): pl.pallas_call(functools.partial(kernel, bands, domains, 0.5 * charge_sca...  55.2 us
    convert_element_type x1, other arithmetic, body(): applied = (potential[None] * values).astype(jnp.bfloat16)  1.87 us
    unnamed x5, local copies, waits for them, and re-layouts  1.26 us

profile of v2, /device:TPU:1, one launch (start us, length us, event | category | flops | bytes accessed | tf_op | source)
XLA Modules:
  0.0 59.0 jit_solution(1260966160331296931)
XLA Ops:
  0.6 0.0 copy-start
  0.6 55.2 %shard_map.77 = f32[4,192,128]{2,1,0:T(8,128)} custom-call(s32[8]{0:T(128)} %occupations.1, bf16[8,4,24576]{2,1,0:T(4,128)(2,1)} %orbitals.1, f32[96,96]{1,0:T(8,128)} %constant.8.clone.left_in, f32[128,128]{1,0:T(8,128)} %constant.9.clone.into_in, f32[128,128]{1,0:T(8,128)} %constant.10.clone.back_in, f32[96,128]{1,0:T(8,128)} %constant.11.clone.weight_in), custom_call_target="tpu_custom_call" | custom-call | tf_op jit(solution)/shard_map/pallas_call | solution.py:570
  55.9 1.3 %copy.10 = f32[1,4,192,128]{3,1,2,0:T(4,128)S(1)} copy(f32[1,4,192,128]{3,2,1,0:T(8,128)} %bitcast.4) | data formatting | bytes 786432
  57.1 0.0 copy-start.1
  57.1 0.0 copy-done
  57.1 1.9 %multiply_convert_fusion = bf16[8,4,24576]{2,1,0:T(4,128)(2,1)} fusion(bf16[8,4,24576]{2,1,0:T(4,128)(2,1)S(1)} %copy-done, f32[4,24576]{1,0:T(4,128)S(1)} %bitcast.5), kind=kLoop, calls=%fused_computation | loop fusion | flops 2359296 | bytes 3538944 | tf_op jit(solution)/shard_map/convert_element_type | solution.py:602
  59.0 0.0 copy-done.1
Async XLA Ops:
  0.6 56.5 %copy-start = (bf16[8,4,24576]{2,1,0:T(4,128)(2,1)S(1)}, bf16[8,4,24576]{2,1,0:T(4,128)(2,1)}, u32[]{:S(2)}) copy-start(bf16[8,4,24576]{2,1,0:T(4,128)(2,1)} %orbitals.1) | copy-start | bytes 4718596
  57.1 1.9 %copy-start.1 = (f32[1,4,192,128]{3,1,2,0:T(4,128)}, f32[1,4,192,128]{3,1,2,0:T(4,128)S(1)}, u32[]{:S(2)}) copy-start(f32[1,4,192,128]{3,1,2,0:T(4,128)S(1)} %copy.10) | copy-start | bytes 1179652

commit v3 on v2

--- a/solution.py
+++ b/solution.py
@@ -23,7 +23,7 @@
 PAD = 8
 CHUNKS = 8
 LAG = 3
-AHEAD = 2
+EARLY = 2
 HALVES = 2
 MOST = (4, 4, 8)
 STEP = NY // CHUNKS
@@ -63,8 +63,10 @@
     out,
     occ, left, into, back, weight, held, mixed, out_s, table_s, held_s,
     acc, from_outer, from_inner, fx, va, vb, vc, hv, t0, t1, t2, t3, g,
+    share, share_outer, share_inner, shares,
     f1, u1a, u1b, f2, u2a, u2b, f3,
     up_s, up_r, mid_s, mid_r, down_s, down_r, near_s, near_r, far_s, far_r, hv_s, hv_r, g_s, g_r,
+    sum_s, sum_r, share_s, share_r, pass_s, pass_r,
 ):
     b = lax.axis_index("band")
     d = lax.axis_index("dom")
@@ -128,6 +130,10 @@
         clear(ref, ref.shape[0] - 1)
     clear(vc, OWN - 2)
     clear(vc, OWN + 5)
+    for p in (OWN - 2, OWN - 1, OWN + 4, OWN + 5):
+        clear(va, p)
+    for p in (OWN - 3, OWN - 2, OWN + 5, OWN + 6):
+        clear(vb, p)
     for k in range(HALO):
         reach = -(-(HALO - k) // PLANES)
 
@@ -151,10 +157,12 @@
             at = first_row + y * PLANES
             mixed[at:at + PLANES, :] = total[:, y * NX:(y + 1) * NX]
         for p in range(PLANES):
-            acc[p, c * STEP:(c + 1) * STEP, :] = mixed[pl.ds(first_row + p, STEP, stride=PLANES), :]
+            plane = mixed[pl.ds(first_row + p, STEP, stride=PLANES), :]
+            acc[p, c * STEP:(c + 1) * STEP, :] = plane
+            va[OWN + p, PAD + c * STEP:PAD + (c + 1) * STEP, :] = plane
 
     tables[0].wait()
-    for c in range(AHEAD):
+    for c in range(CHUNKS):
         density(c)
     pl.semaphore_wait(barrier, domains + jnp.where(has_outer, 1, 0))
 
@@ -219,9 +227,6 @@
 
     def gathered(c, at_centre):
         rows = slice(c * STEP, (c + 1) * STEP)
-
-        if c >= AHEAD:
-            density(c)
 
         @pl.when(has_outer)
         def _():
@@ -258,30 +263,6 @@
                 def _():
                     far_copy(i, c // (CHUNKS // HALVES)).start()
 
-    @pl.when(centre)
-    def _():
-        for c in range(CHUNKS + LAG):
-            if c < CHUNKS:
-                gathered(c, True)
-            if c >= LAG:
-                spread(c - LAG, True)
-
-    @pl.when(jnp.logical_not(centre))
-    def _():
-        for c in range(CHUNKS):
-            gathered(c, False)
-        for c in range(CHUNKS):
-            spread(c, False)
-
-    for c in range(CHUNKS):
-        @pl.when(d < domains - 1)
-        def _():
-            near_down(c).wait_recv()
-
-        @pl.when(d > 0)
-        def _():
-            near_up(c).wait_recv()
-
     def beside(src, p, r0, rn, width):
         c = src[p, PAD + r0:PAD + r0 + rn, :]
         lane = lax.broadcasted_iota(jnp.int32, (rn, NX), 1)
@@ -364,14 +345,106 @@
             g.at[cycle, origin], g.at[cycle, origin], g_s.at[cycle, i], g_r.at[cycle, i], (b, origin)
         )
 
+    def packed(v, source, at, to):
+        a = pooled(v, source, 0, at, t0)
+        a = a + pltpu.roll(a, NX - 1, 1)
+        e = pooled(v, source, 0, to, t1)
+        e = e + pltpu.roll(e, 1, 1)
+        return 0.5 * jnp.where(even, a, e)
+
     def restrict_and_send(v, cycle):
-        a = pooled(v, fx, 0, OWN, t0)
-        a = a + pltpu.roll(a, NX - 1, 1)
-        e = pooled(v, fx, 0, OWN + 2, t1)
-        e = e + pltpu.roll(e, 1, 1)
-        g[cycle, d] = 0.5 * jnp.where(even, a, e)
+        g[cycle, d] = packed(v, fx, OWN, OWN + 2)
         for i in range(1, domains):
             give(cycle, i).start()
+
+    sibling = d + 1 - 2 * lax.rem(d, 2)
+    chips = domains // 2
+
+    def sum_up():
+        return remote(share, share_outer, sum_s.at[0], sum_r.at[0], (inner, d))
+
+    def sum_mid():
+        return remote(share, share_inner, sum_s.at[1], sum_r.at[1], (inner, d))
+
+    def sum_down(dev):
+        return remote(shares.at[d], shares.at[d], sum_s.at[2], sum_r.at[2], (dev, d))
+
+    def tell(i):
+        dev = sibling if i == 0 else lax.rem(d + 2 * i, domains)
+        return remote(shares.at[d], shares.at[d], share_s.at[i], share_r.at[i], (b, dev))
+
+    def told(i):
+        origin = sibling if i == 0 else lax.rem(d + (domains - 2 * i), domains)
+        return remote(shares.at[origin], shares.at[origin], share_s.at[i], share_r.at[i], (b, origin))
+
+    def hand_on(i):
+        origin = lax.rem(d + (domains - 2 * i), domains)
+        return remote(shares.at[origin], shares.at[origin], pass_s.at[i], pass_r.at[i], (b, sibling))
+
+    def handed(i):
+        origin = lax.rem(sibling + (domains - 2 * i), domains)
+        return remote(shares.at[origin], shares.at[origin], pass_s.at[i], pass_r.at[i], (b, sibling))
+
+    def make_share():
+        first(va, vb, 0, *window(1))
+        share[0] = packed(vb, va, OWN, OWN + 2)
+        share[1] = packed(vb, va, OWN - 2, OWN + 4)
+
+    def gather_share(at_centre):
+        @pl.when(has_outer)
+        def _():
+            sum_up().wait_recv()
+            share[...] = share[...] + share_outer[...]
+
+        (sum_mid() if at_centre else sum_up()).start()
+
+    def spread_share(at_centre):
+        if at_centre:
+            sum_mid().wait_recv()
+            shares[d] = share[...] + share_inner[...]
+        else:
+            sum_down(inner).wait_recv()
+
+        @pl.when(has_outer)
+        def _():
+            sum_down(outer).start()
+
+        for i in range(chips):
+            tell(i).start()
+
+    order = list(range(EARLY)) + [None] + list(range(EARLY, CHUNKS))
+
+    def gather_step(n, at_centre):
+        if order[n] is None:
+            gather_share(at_centre)
+        else:
+            gathered(order[n], at_centre)
+
+    def spread_step(n, at_centre):
+        if order[n] is None:
+            spread_share(at_centre)
+        else:
+            spread(order[n], at_centre)
+
+    def total_share(e, j):
+        below = shares[jnp.maximum(e - 1, 0), 1] * jnp.where(e > 0, 1.0, 0.0)
+        above = shares[jnp.minimum(e + 1, domains - 1), 1] * jnp.where(e < domains - 1, 1.0, 0.0)
+        a = shares[e, 0] + jnp.where(even, pltpu.roll(below, NX - 1, 1), pltpu.roll(above, 1, 1))
+        f1[1 + 2 * e, PAD:PAD + rows1, :] = jnp.where(even, a, pltpu.roll(a, 1, 1))
+        f1[2 + 2 * e, PAD:PAD + rows1, :] = jnp.where(even, pltpu.roll(a, NX - 1, 1), a)
+
+    def gathered_shares():
+        told(0).wait_recv()
+        for i in range(1, chips):
+            handed(i).wait_recv()
+        loop(0, domains, total_share, 2)
+
+    def gathered_residuals():
+        unpack(1, d)
+        for i in range(1, domains):
+            origin, copy = take(1, i)
+            copy.wait_recv()
+            unpack(1, origin)
 
     def unpack(cycle, origin):
         a = g[cycle, origin]
@@ -389,18 +462,15 @@
             at = (p, pl.ds(PAD + odd, n, stride=2), slice(None))
             dst[at] = dst[at] + value
 
-    def coarse(cycle, near):
-        unpack(cycle, d)
-        for i in range(1, domains):
-            origin, copy = take(cycle, i)
-            copy.wait_recv()
-            unpack(cycle, origin)
+    def coarse(arrive, near, between):
+        arrive()
         first(f1, u1a, 1, 1, n1)
 
         def down1(q, j):
             f2[1 + q, PAD:PAD + NY // 4, :] = widen(pooled(u1a, f1, 1, 1 + 2 * q, spare[j]), 1)
 
         loop(0, n2, down1)
+        between()
         first(f2, u2a, 2, 1, n2)
         rows3 = NY // 8
 
@@ -445,17 +515,53 @@
                 add_rows(v, w, value, rows1)
                 add_rows(v, w + 1, value, rows1)
 
-    for i in range(2):
-        @pl.when(onward[i][4])
-        def _():
-            for h in range(HALVES):
-                onward_copy(i, h).start()
-
+    @pl.when(jnp.logical_not(centre))
+    def _():
+        for n in range(EARLY):
+            gather_step(n, False)
+
+    make_share()
+
+    @pl.when(centre)
+    def _():
+        for n in range(len(order) + LAG):
+            if n < len(order):
+                gather_step(n, True)
+            if n >= LAG:
+                spread_step(n - LAG, True)
+
+    @pl.when(jnp.logical_not(centre))
+    def _():
+        for n in range(EARLY, len(order)):
+            gather_step(n, False)
+        for n in range(len(order)):
+            spread_step(n, False)
+
+    for i in range(1, chips):
+        told(i).wait_recv()
+        hand_on(i).start()
+
+    def near_arrived():
+        for c in range(CHUNKS):
+            @pl.when(d < domains - 1)
+            def _():
+                near_down(c).wait_recv()
+
+            @pl.when(d > 0)
+            def _():
+                near_up(c).wait_recv()
+
+        for i in range(2):
+            @pl.when(onward[i][4])
+            def _():
+                for h in range(HALVES):
+                    onward_copy(i, h).start()
+
+        for table in tables[1:]:
+            table.wait()
+
+    coarse(gathered_shares, 3, near_arrived)
     first(fx, vb, 0, *window(1))
-    restrict_and_send(vb, 0)
-    for table in tables[1:]:
-        table.wait()
-    coarse(0, 3)
 
     for i in range(4):
         @pl.when(far[i][4])
@@ -491,7 +597,7 @@
     def _():
         v_down().start()
 
-    coarse(1, 1)
+    coarse(gathered_residuals, 1, lambda: None)
 
     @pl.when(d < domains - 1)
     def _():
@@ -550,9 +656,24 @@
             for h in range(HALVES):
                 onward_copy(i, h).wait_send()
 
-    for cycle in range(2):
-        for i in range(1, domains):
-            give(cycle, i).wait_send()
+    for i in range(chips):
+        tell(i).wait_send()
+    for i in range(1, chips):
+        hand_on(i).wait_send()
+    for i in range(1, domains):
+        give(1, i).wait_send()
+
+    @pl.when(centre)
+    def _():
+        sum_mid().wait_send()
+
+    @pl.when(jnp.logical_not(centre))
+    def _():
+        sum_up().wait_send()
+
+    @pl.when(has_outer)
+    def _():
+        sum_down(outer).wait_send()
 
 
 def potential_of(orbitals, occupations, bands, domains):
@@ -560,12 +681,15 @@
     tables = coarse_basis(n3)
     f32 = jnp.float32
     count = orbitals.shape[0]
+    pair = pltpu.VMEM((2, NY // 2, NX), f32)
     slab = pltpu.VMEM((PLANES, NY, NX), f32)
     fine = pltpu.VMEM((WINDOW, NY + 2 * PAD, NX), f32)
     level1 = pltpu.VMEM((n1 + 2, NY // 2 + 2 * PAD, NX), f32)
     level2 = pltpu.VMEM((n2 + 2, NY // 4 + 2 * PAD, NX), f32)
     chunk_sems = pltpu.SemaphoreType.DMA((CHUNKS,))
     near_sems = pltpu.SemaphoreType.DMA((2, CHUNKS))
+    sum_sems = pltpu.SemaphoreType.DMA((3,))
+    chip_sems = pltpu.SemaphoreType.DMA((domains // 2,))
     gather_sems = pltpu.SemaphoreType.DMA((2, domains))
     return pl.pallas_call(
         functools.partial(kernel, bands, domains, 0.5 * charge_scale / (count * bands)),
@@ -582,6 +706,7 @@
             pltpu.VMEM((2, 2, NY, NX), f32),
             *[pltpu.VMEM((NY, NX), f32)] * 4,
             pltpu.VMEM((2, domains, NY // 2, NX), f32),
+            pair, pair, pair, pltpu.VMEM((domains, 2, NY // 2, NX), f32),
             level1, level1, level1, level2, level2, level2,
             pltpu.VMEM((n3 * (NY // 8), NX), f32),
             chunk_sems, chunk_sems, chunk_sems, chunk_sems, chunk_sems, chunk_sems,
@@ -589,6 +714,7 @@
             pltpu.SemaphoreType.DMA((6, HALVES)), pltpu.SemaphoreType.DMA((4, HALVES)),
             pltpu.SemaphoreType.DMA((2,)), pltpu.SemaphoreType.DMA((2,)),
             gather_sems, gather_sems,
+            sum_sems, sum_sems, chip_sems, chip_sems, chip_sems, chip_sems,
         ],
         compiler_params=pltpu.CompilerParams(
             collective_id=0, has_side_effects=True, vmem_limit_bytes=62_500_000

time: 59.2 us -> 56.5 us (0.954)
  Pallas kernels: 55.2 us -> 52.5 us
    pallas_call x1, Pallas kernels: 55.2 us -> 52.5 us  [potential_of(): pl.pallas_call(functools.partial(kernel, bands, domains, 0.5 * charge_sca...]
where the time goes in v3:
time: 56.5 us; the launch traced here: 56.3 us
  Pallas kernels  52.5 us (93%)
  other arithmetic  1.87 us (3%)
  local copies, waits for them, and re-layouts  1.26 us (2%)
  between operations  0.66 us (1%)
    pallas_call x1, Pallas kernels, potential_of(): pl.pallas_call(functools.partial(kernel, bands, domains, 0.5 * charge_sca...  52.5 us
    convert_element_type x1, other arithmetic, body(): applied = (potential[None] * values).astype(jnp.bfloat16)  1.87 us
    unnamed x5, local copies, waits for them, and re-layouts  1.26 us

profile of v3, /device:TPU:1, one launch (start us, length us, event | category | flops | bytes accessed | tf_op | source)
XLA Modules:
  0.0 56.3 jit_solution(17580156047144587832)
XLA Ops:
  0.6 0.0 copy-start
  0.6 52.5 %shard_map.77 = f32[4,192,128]{2,1,0:T(8,128)} custom-call(s32[8]{0:T(128)} %occupations.1, bf16[8,4,24576]{2,1,0:T(4,128)(2,1)} %orbitals.1, f32[96,96]{1,0:T(8,128)} %constant.8.clone.left_in, f32[128,128]{1,0:T(8,128)} %constant.9.clone.into_in, f32[128,128]{1,0:T(8,128)} %constant.10.clone.back_in, f32[96,128]{1,0:T(8,128)} %constant.11.clone.weight_in), custom_call_target="tpu_custom_call" | custom-call | tf_op jit(solution)/shard_map/pallas_call | solution.py:694
  53.2 1.3 %copy.10 = f32[1,4,192,128]{3,1,2,0:T(4,128)S(1)} copy(f32[1,4,192,128]{3,2,1,0:T(8,128)} %bitcast.4) | data formatting | bytes 786432
  54.4 0.0 copy-start.1
  54.4 0.0 copy-done
  54.5 1.9 %multiply_convert_fusion = bf16[8,4,24576]{2,1,0:T(4,128)(2,1)} fusion(bf16[8,4,24576]{2,1,0:T(4,128)(2,1)S(1)} %copy-done, f32[4,24576]{1,0:T(4,128)S(1)} %bitcast.5), kind=kLoop, calls=%fused_computation | loop fusion | flops 2359296 | bytes 3538944 | tf_op jit(solution)/shard_map/convert_element_type | solution.py:728
  56.3 0.0 copy-done.1
Async XLA Ops:
  0.6 53.8 %copy-start = (bf16[8,4,24576]{2,1,0:T(4,128)(2,1)S(1)}, bf16[8,4,24576]{2,1,0:T(4,128)(2,1)}, u32[]{:S(2)}) copy-start(bf16[8,4,24576]{2,1,0:T(4,128)(2,1)} %orbitals.1) | copy-start | bytes 4718596
  54.4 1.9 %copy-start.1 = (f32[1,4,192,128]{3,1,2,0:T(4,128)}, f32[1,4,192,128]{3,1,2,0:T(4,128)S(1)}, u32[]{:S(2)}) copy-start(f32[1,4,192,128]{3,1,2,0:T(4,128)S(1)} %copy.10) | copy-start | bytes 1179652

commit v4 on v3

--- a/solution.py
+++ b/solution.py
@@ -65,7 +65,7 @@
     acc, from_outer, from_inner, fx, va, vb, vc, hv, t0, t1, t2, t3, g,
     share, share_outer, share_inner, shares,
     f1, u1a, u1b, f2, u2a, u2b, f3,
-    up_s, up_r, mid_s, mid_r, down_s, down_r, near_s, near_r, far_s, far_r, hv_s, hv_r, g_s, g_r,
+    up_s, up_r, mid_s, mid_r, down_s, down_r, near_s, near_r, far_s, far_r, hv_s, hv_r,
     sum_s, sum_r, share_s, share_r, pass_s, pass_r,
 ):
     b = lax.axis_index("band")
@@ -91,7 +91,8 @@
         return pltpu.make_async_copy(orbitals.at[at], held.at[at], held_s.at[c])
 
     def result(p):
-        return pltpu.make_async_copy(acc.at[p], out.at[p], out_s.at[p])
+        rows = pl.ds(p * NY, NY)
+        return pltpu.make_async_copy(mixed.at[rows], out.at[rows], out_s.at[p])
 
     tables = [
         pltpu.make_async_copy(src, dst, table_s.at[i])
@@ -333,18 +334,6 @@
     rows1 = NY // 2
     even = lax.broadcasted_iota(jnp.int32, (rows1, NX), 1) % 2 == 0
 
-    def give(cycle, i):
-        return remote(
-            g.at[cycle, d], g.at[cycle, d], g_s.at[cycle, i], g_r.at[cycle, i],
-            (b, lax.rem(d + i, domains)),
-        )
-
-    def take(cycle, i):
-        origin = lax.rem(d + (domains - i), domains)
-        return origin, remote(
-            g.at[cycle, origin], g.at[cycle, origin], g_s.at[cycle, i], g_r.at[cycle, i], (b, origin)
-        )
-
     def packed(v, source, at, to):
         a = pooled(v, source, 0, at, t0)
         a = a + pltpu.roll(a, NX - 1, 1)
@@ -354,8 +343,9 @@
 
     def restrict_and_send(v, cycle):
         g[cycle, d] = packed(v, fx, OWN, OWN + 2)
-        for i in range(1, domains):
-            give(cycle, i).start()
+        for i in range(1, chips):
+            tell(i, cycle).start()
+        tell(0, cycle).start()
 
     sibling = d + 1 - 2 * lax.rem(d, 2)
     chips = domains // 2
@@ -369,21 +359,29 @@
     def sum_down(dev):
         return remote(shares.at[d], shares.at[d], sum_s.at[2], sum_r.at[2], (dev, d))
 
-    def tell(i):
+    def block(cycle, origin):
+        return g.at[1, origin] if cycle else shares.at[origin]
+
+    def tell(i, cycle):
         dev = sibling if i == 0 else lax.rem(d + 2 * i, domains)
-        return remote(shares.at[d], shares.at[d], share_s.at[i], share_r.at[i], (b, dev))
-
-    def told(i):
-        origin = sibling if i == 0 else lax.rem(d + (domains - 2 * i), domains)
-        return remote(shares.at[origin], shares.at[origin], share_s.at[i], share_r.at[i], (b, origin))
-
-    def hand_on(i):
-        origin = lax.rem(d + (domains - 2 * i), domains)
-        return remote(shares.at[origin], shares.at[origin], pass_s.at[i], pass_r.at[i], (b, sibling))
-
-    def handed(i):
-        origin = lax.rem(sibling + (domains - 2 * i), domains)
-        return remote(shares.at[origin], shares.at[origin], pass_s.at[i], pass_r.at[i], (b, sibling))
+        src = block(cycle, d)
+        return remote(src, src, share_s.at[cycle, i], share_r.at[cycle, i], (b, dev))
+
+    def origin_of(i, near):
+        return sibling if i == 0 else lax.rem(near + (domains - 2 * i), domains)
+
+    def told(i, cycle):
+        origin = origin_of(i, d)
+        src = block(cycle, origin)
+        return remote(src, src, share_s.at[cycle, i], share_r.at[cycle, i], (b, origin))
+
+    def hand_on(i, cycle):
+        src = block(cycle, origin_of(i, d))
+        return remote(src, src, pass_s.at[cycle, i], pass_r.at[cycle, i], (b, sibling))
+
+    def handed(i, cycle):
+        src = block(cycle, origin_of(i, sibling))
+        return remote(src, src, pass_s.at[cycle, i], pass_r.at[cycle, i], (b, sibling))
 
     def make_share():
         first(va, vb, 0, *window(1))
@@ -410,7 +408,7 @@
             sum_down(outer).start()
 
         for i in range(chips):
-            tell(i).start()
+            tell(i, 0).start()
 
     order = list(range(EARLY)) + [None] + list(range(EARLY, CHUNKS))
 
@@ -434,17 +432,23 @@
         f1[2 + 2 * e, PAD:PAD + rows1, :] = jnp.where(even, pltpu.roll(a, NX - 1, 1), a)
 
     def gathered_shares():
-        told(0).wait_recv()
+        told(0, 0).wait_recv()
         for i in range(1, chips):
-            handed(i).wait_recv()
+            handed(i, 0).wait_recv()
         loop(0, domains, total_share, 2)
 
     def gathered_residuals():
+        for i in range(1, chips):
+            told(i, 1).wait_recv()
+            hand_on(i, 1).start()
         unpack(1, d)
-        for i in range(1, domains):
-            origin, copy = take(1, i)
-            copy.wait_recv()
-            unpack(1, origin)
+        for i in range(1, chips):
+            unpack(1, origin_of(i, d))
+        told(0, 1).wait_recv()
+        unpack(1, sibling)
+        for i in range(1, chips):
+            handed(i, 1).wait_recv()
+            unpack(1, origin_of(i, sibling))
 
     def unpack(cycle, origin):
         a = g[cycle, origin]
@@ -538,8 +542,8 @@
             spread_step(n, False)
 
     for i in range(1, chips):
-        told(i).wait_recv()
-        hand_on(i).start()
+        told(i, 0).wait_recv()
+        hand_on(i, 0).start()
 
     def near_arrived():
         for c in range(CHUNKS):
@@ -622,14 +626,14 @@
 
     correct(vc, 1)
     sweep(vc, fx, va, 0, *window(1))
-    for p in range(PLANES):
-        for r0, rn in blocks(0):
+    for k, (r0, rn) in enumerate(blocks(0)):
+        for p in range(PLANES):
             c, total = beside(va, OWN + p, r0, rn, 1)
             f = fx[OWN + p, PAD + r0:PAD + r0 + rn, :]
-            acc[p, r0:r0 + rn, :] = KEEP * c + GAIN[0] * (f + total)
-        result(p).start()
-    for p in range(PLANES):
-        result(p).wait()
+            mixed[pl.ds(r0 * PLANES + p, rn, stride=PLANES), :] = KEEP * c + GAIN[0] * (f + total)
+        result(k).start()
+    for k in range(4):
+        result(k).wait()
 
     for c in range(CHUNKS):
         @pl.when(has_outer)
@@ -656,12 +660,11 @@
             for h in range(HALVES):
                 onward_copy(i, h).wait_send()
 
-    for i in range(chips):
-        tell(i).wait_send()
-    for i in range(1, chips):
-        hand_on(i).wait_send()
-    for i in range(1, domains):
-        give(1, i).wait_send()
+    for cycle in range(2):
+        for i in range(chips):
+            tell(i, cycle).wait_send()
+        for i in range(1, chips):
+            hand_on(i, cycle).wait_send()
 
     @pl.when(centre)
     def _():
@@ -689,11 +692,10 @@
     chunk_sems = pltpu.SemaphoreType.DMA((CHUNKS,))
     near_sems = pltpu.SemaphoreType.DMA((2, CHUNKS))
     sum_sems = pltpu.SemaphoreType.DMA((3,))
-    chip_sems = pltpu.SemaphoreType.DMA((domains // 2,))
-    gather_sems = pltpu.SemaphoreType.DMA((2, domains))
+    chip_sems = pltpu.SemaphoreType.DMA((2, domains // 2))
     return pl.pallas_call(
         functools.partial(kernel, bands, domains, 0.5 * charge_scale / (count * bands)),
-        out_shape=jax.ShapeDtypeStruct((PLANES, NY, NX), f32),
+        out_shape=jax.ShapeDtypeStruct((NY * PLANES, NX), f32),
         in_specs=[pl.BlockSpec(memory_space=pl.ANY)] * 6,
         out_specs=pl.BlockSpec(memory_space=pl.ANY),
         scratch_shapes=[
@@ -713,7 +715,6 @@
             near_sems, near_sems,
             pltpu.SemaphoreType.DMA((6, HALVES)), pltpu.SemaphoreType.DMA((4, HALVES)),
             pltpu.SemaphoreType.DMA((2,)), pltpu.SemaphoreType.DMA((2,)),
-            gather_sems, gather_sems,
             sum_sems, sum_sems, chip_sems, chip_sems, chip_sems, chip_sems,
         ],
         compiler_params=pltpu.CompilerParams(
@@ -722,11 +723,68 @@
     )(occupations, orbitals, *[jnp.asarray(table) for table in tables])
 
 
+def apply(mixed_in, orbitals, potential, applied, mixed, flat, held, in_s, orb_s, flat_s, held_s):
+    rows, lanes = STEP * PLANES, STEP * NX
+
+    def fetch(c):
+        at = pl.ds(c * rows, rows)
+        return pltpu.make_async_copy(mixed_in.at[at], mixed.at[at], in_s.at[c])
+
+    def read(c):
+        at = (slice(None), slice(None), pl.ds(c * lanes, lanes))
+        return pltpu.make_async_copy(orbitals.at[at], held.at[at], orb_s.at[c])
+
+    def keep(c):
+        at = (slice(None), pl.ds(c * lanes, lanes))
+        return pltpu.make_async_copy(flat.at[at], potential.at[at], flat_s.at[c])
+
+    def store(c):
+        at = (slice(None), slice(None), pl.ds(c * lanes, lanes))
+        return pltpu.make_async_copy(held.at[at], applied.at[at], held_s.at[c])
+
+    for c in range(CHUNKS):
+        fetch(c).start()
+        read(c).start()
+    for c in range(CHUNKS):
+        fetch(c).wait()
+        for y in range(c * STEP, (c + 1) * STEP):
+            flat[:, y * NX:(y + 1) * NX] = mixed[y * PLANES:(y + 1) * PLANES, :]
+        keep(c).start()
+        value = flat[:, c * lanes:(c + 1) * lanes]
+        read(c).wait()
+        for i in range(orbitals.shape[0]):
+            psi = held[i, :, c * lanes:(c + 1) * lanes].astype(jnp.float32)
+            held[i, :, c * lanes:(c + 1) * lanes] = (value * psi).astype(held.dtype)
+        store(c).start()
+    for c in range(CHUNKS):
+        keep(c).wait()
+        store(c).wait()
+
+
+def applied_of(mixed, orbitals):
+    flat = (PLANES, NY * NX)
+    sems = pltpu.SemaphoreType.DMA((CHUNKS,))
+    anywhere = pl.BlockSpec(memory_space=pl.ANY)
+    return pl.pallas_call(
+        apply,
+        out_shape=(
+            jax.ShapeDtypeStruct(flat, jnp.float32),
+            jax.ShapeDtypeStruct(orbitals.shape, orbitals.dtype),
+        ),
+        in_specs=[anywhere, anywhere],
+        out_specs=(anywhere, anywhere),
+        scratch_shapes=[
+            pltpu.VMEM((NY * PLANES, NX), jnp.float32),
+            pltpu.VMEM(flat, jnp.float32),
+            pltpu.VMEM(orbitals.shape, orbitals.dtype),
+            sems, sems, sems, sems,
+        ],
+        compiler_params=pltpu.CompilerParams(vmem_limit_bytes=62_500_000),
+    )(mixed, orbitals)
+
+
 def body(bands, domains, orbitals, occupations):
-    values = orbitals.astype(jnp.float32)
-    potential = potential_of(orbitals, occupations, bands, domains).reshape(orbitals.shape[1], NY * NX)
-    applied = (potential[None] * values).astype(jnp.bfloat16)
-    return (potential, applied)
+    return applied_of(potential_of(orbitals, occupations, bands, domains), orbitals)
 
 
 def solution(mesh):

time: 56.5 us -> 54.5 us (0.965); the launches traced: 56.3 us -> 53.7 us
  other arithmetic: 1.87 us -> 0 us
  local copies, waits for them, and re-layouts: 1.26 us -> 0 us
    pallas_call x0 -> x1, Pallas kernels: none -> 2.66 us  [applied_of(): pl.pallas_call(apply, out_shape=(jax.ShapeDtypeStruct(flat, jnp.float32),...]
    pallas_call x1, Pallas kernels: 52.5 us -> 50.4 us  [potential_of(): pl.pallas_call(functools.partial(kernel, bands, domains, 0.5 * charge_sca...]
    convert_element_type x1 -> x0, other arithmetic: 1.87 us -> none  [body(): applied = (potential[None] * values).astype(jnp.bfloat16)]
    unnamed x5 -> x0, local copies, waits for them, and re-layouts: 1.26 us -> none
where the time goes in v4:
time: 54.5 us; the launch traced here: 53.7 us
  Pallas kernels  53 us (97%)
  between operations  0.64 us (1%)
    pallas_call x1, Pallas kernels, potential_of(): pl.pallas_call(functools.partial(kernel, bands, domains, 0.5 * charge_sca...  50.4 us
    pallas_call x1, Pallas kernels, applied_of(): pl.pallas_call(apply, out_shape=(jax.ShapeDtypeStruct(flat, jnp.float32),...  2.66 us

profile of v4, /device:TPU:1, one launch (start us, length us, event | category | flops | bytes accessed | tf_op | source)
XLA Modules:
  0.0 53.7 jit_solution(16268376800892830811)
XLA Ops:
  0.6 50.4 %shard_map.77.mixed_in = f32[768,128]{1,0:T(8,128)} custom-call(s32[8]{0:T(128)} %occupations.1, bf16[8,4,24576]{2,1,0:T(4,128)(2,1)} %orbitals.3, f32[96,96]{1,0:T(8,128)} %constant.8.clone.left_in, f32[128,128]{1,0:T(8,128)} %constant.9.clone.into_in, f32[128,128]{1,0:T(8,128)} %constant.10.clone.back_in, f32[96,128]{1,0:T(8,128)} %constant.11.clone.weight_in), custom_call_target="tpu_custom_call" | custom-call | tf_op jit(solution)/shard_map/pallas_call | solution.py:696
  51.0 2.7 %shard_map.78 = (f32[4,24576]{1,0:T(4,128)}, bf16[8,4,24576]{2,1,0:T(4,128)(2,1)}) custom-call(f32[768,128]{1,0:T(8,128)} %shard_map.77.mixed_in, bf16[8,4,24576]{2,1,0:T(4,128)(2,1)} %orbitals.3), custom_call_target="tpu_custom_call" | custom-call | tf_op jit(solution)/shard_map/pallas_call | solution.py:768

commit v5 on v4

--- a/solution.py
+++ b/solution.py
@@ -24,6 +24,7 @@
 CHUNKS = 8
 LAG = 3
 EARLY = 2
+ROOM = 8192
 HALVES = 2
 MOST = (4, 4, 8)
 STEP = NY // CHUNKS
@@ -84,14 +85,15 @@
             device_id=dev, device_id_type=pl.DeviceIdType.MESH,
         )
 
-    lanes = STEP * NX
+    lines = STEP * PLANES
 
     def fetch(c):
-        at = (slice(None), slice(None), pl.ds(c * lanes, lanes))
+        at = (slice(None), pl.ds(c * lines, lines), slice(None))
         return pltpu.make_async_copy(orbitals.at[at], held.at[at], held_s.at[c])
 
     def result(p):
-        rows = pl.ds(p * NY, NY)
+        r0, rn = blocks(0)[p]
+        rows = pl.ds(r0 * PLANES, rn * PLANES)
         return pltpu.make_async_copy(mixed.at[rows], out.at[rows], out_s.at[p])
 
     tables = [
@@ -148,22 +150,20 @@
 
     def density(c):
         fetch(c).wait()
+        first_row = c * lines
         total = None
         for i in range(orbitals.shape[0]):
-            value = held[i, :, c * lanes:(c + 1) * lanes].astype(jnp.float32)
+            value = held[i, first_row:first_row + lines, :].astype(jnp.float32)
             term = (occ[i].astype(jnp.float32) * scale) * (value * value)
             total = term if total is None else total + term
-        first_row = c * STEP * PLANES
-        for y in range(STEP):
-            at = first_row + y * PLANES
-            mixed[at:at + PLANES, :] = total[:, y * NX:(y + 1) * NX]
+        mixed[first_row:first_row + lines, :] = total
         for p in range(PLANES):
             plane = mixed[pl.ds(first_row + p, STEP, stride=PLANES), :]
             acc[p, c * STEP:(c + 1) * STEP, :] = plane
             va[OWN + p, PAD + c * STEP:PAD + (c + 1) * STEP, :] = plane
 
     tables[0].wait()
-    for c in range(CHUNKS):
+    for c in range(EARLY):
         density(c)
     pl.semaphore_wait(barrier, domains + jnp.where(has_outer, 1, 0))
 
@@ -508,22 +508,22 @@
             start = jnp.clip(2 * d - near - extra, 0, n1 - count)
             sweep(src, f1, dst, 1, start + 1, count)
 
-    def correct(v, near):
-        for j in range(-near, 2 + near):
+    def correct(v, planes):
+        for p in planes:
+            j = (p - OWN) // 2
             z = 2 * d + j
-            w = 2 * j + OWN
 
             @pl.when(jnp.logical_and(z >= 0, z < n1))
             def _():
-                value = u1a[z + 1, PAD:PAD + rows1, :]
-                add_rows(v, w, value, rows1)
-                add_rows(v, w + 1, value, rows1)
+                add_rows(v, p, u1a[z + 1, PAD:PAD + rows1, :], rows1)
 
     @pl.when(jnp.logical_not(centre))
     def _():
         for n in range(EARLY):
             gather_step(n, False)
 
+    for c in range(EARLY, CHUNKS):
+        density(c)
     make_share()
 
     @pl.when(centre)
@@ -566,6 +566,8 @@
 
     coarse(gathered_shares, 3, near_arrived)
     first(fx, vb, 0, *window(1))
+    correct(vb, range(OWN - 1, OWN + 5))
+    sweep(vb, fx, va, 0, *window(0))
 
     for i in range(4):
         @pl.when(far[i][4])
@@ -575,8 +577,9 @@
 
     first(fx, vb, 0, OWN - 5, 4)
     first(fx, vb, 0, OWN + PLANES + 1, 4)
-    correct(vb, 3)
-    sweep(vb, fx, va, 0, *window(4))
+    correct(vb, [*range(OWN - 5, OWN - 1), *range(OWN + 5, OWN + 9)])
+    sweep(vb, fx, va, 0, OWN - 4, 4)
+    sweep(vb, fx, va, 0, OWN + 4, 4)
     sweep(va, fx, vb, 0, *window(3))
 
     sweep(vb, fx, va, 0, *window(2))
@@ -624,7 +627,7 @@
         def _():
             up(c).wait_send()
 
-    correct(vc, 1)
+    correct(vc, range(OWN - 2, OWN + 6))
     sweep(vc, fx, va, 0, *window(1))
     for k, (r0, rn) in enumerate(blocks(0)):
         for p in range(PLANES):
@@ -632,7 +635,7 @@
             f = fx[OWN + p, PAD + r0:PAD + r0 + rn, :]
             mixed[pl.ds(r0 * PLANES + p, rn, stride=PLANES), :] = KEEP * c + GAIN[0] * (f + total)
         result(k).start()
-    for k in range(4):
+    for k in range(len(blocks(0))):
         result(k).wait()
 
     for c in range(CHUNKS):
@@ -695,7 +698,7 @@
     chip_sems = pltpu.SemaphoreType.DMA((2, domains // 2))
     return pl.pallas_call(
         functools.partial(kernel, bands, domains, 0.5 * charge_scale / (count * bands)),
-        out_shape=jax.ShapeDtypeStruct((NY * PLANES, NX), f32),
+        out_shape=jax.ShapeDtypeStruct((ROOM, NX), f32),
         in_specs=[pl.BlockSpec(memory_space=pl.ANY)] * 6,
         out_specs=pl.BlockSpec(memory_space=pl.ANY),
         scratch_shapes=[
@@ -703,7 +706,7 @@
             *[pltpu.VMEM(table.shape, f32) for table in tables],
             pltpu.VMEM(orbitals.shape, orbitals.dtype),
             pltpu.VMEM((NY * PLANES, NX), f32),
-            pltpu.SemaphoreType.DMA((PLANES,)), pltpu.SemaphoreType.DMA((5,)), chunk_sems,
+            pltpu.SemaphoreType.DMA((8,)), pltpu.SemaphoreType.DMA((5,)), chunk_sems,
             slab, slab, slab, fine, fine, fine, fine,
             pltpu.VMEM((2, 2, NY, NX), f32),
             *[pltpu.VMEM((NY, NX), f32)] * 4,
@@ -723,68 +726,71 @@
     )(occupations, orbitals, *[jnp.asarray(table) for table in tables])
 
 
-def apply(mixed_in, orbitals, potential, applied, mixed, flat, held, in_s, orb_s, flat_s, held_s):
-    rows, lanes = STEP * PLANES, STEP * NX
+def apply(mixed_in, orbitals, potential, applied, mixed, held, in_s, keep_s, held_s):
+    rows = STEP * PLANES
+
+    def part(c):
+        return (slice(None), pl.ds(c * rows, rows), slice(None))
 
     def fetch(c):
         at = pl.ds(c * rows, rows)
         return pltpu.make_async_copy(mixed_in.at[at], mixed.at[at], in_s.at[c])
 
-    def read(c):
-        at = (slice(None), slice(None), pl.ds(c * lanes, lanes))
-        return pltpu.make_async_copy(orbitals.at[at], held.at[at], orb_s.at[c])
-
     def keep(c):
-        at = (slice(None), pl.ds(c * lanes, lanes))
-        return pltpu.make_async_copy(flat.at[at], potential.at[at], flat_s.at[c])
+        at = pl.ds(c * rows, rows)
+        return pltpu.make_async_copy(mixed.at[at], potential.at[at], keep_s.at[c])
 
     def store(c):
-        at = (slice(None), slice(None), pl.ds(c * lanes, lanes))
-        return pltpu.make_async_copy(held.at[at], applied.at[at], held_s.at[c])
+        return pltpu.make_async_copy(held.at[part(c)], applied.at[part(c)], held_s.at[c])
 
     for c in range(CHUNKS):
         fetch(c).start()
-        read(c).start()
     for c in range(CHUNKS):
         fetch(c).wait()
-        for y in range(c * STEP, (c + 1) * STEP):
-            flat[:, y * NX:(y + 1) * NX] = mixed[y * PLANES:(y + 1) * PLANES, :]
         keep(c).start()
-        value = flat[:, c * lanes:(c + 1) * lanes]
-        read(c).wait()
+        value = mixed[c * rows:(c + 1) * rows, :]
         for i in range(orbitals.shape[0]):
-            psi = held[i, :, c * lanes:(c + 1) * lanes].astype(jnp.float32)
-            held[i, :, c * lanes:(c + 1) * lanes] = (value * psi).astype(held.dtype)
+            psi = orbitals[i, c * rows:(c + 1) * rows, :].astype(jnp.float32)
+            held[i, c * rows:(c + 1) * rows, :] = (value * psi).astype(held.dtype)
         store(c).start()
     for c in range(CHUNKS):
         keep(c).wait()
         store(c).wait()
 
 
-def applied_of(mixed, orbitals):
-    flat = (PLANES, NY * NX)
+def cells_of(orbitals):
+    count = orbitals.shape[0]
+    cells = orbitals.reshape(count, PLANES, NY, NX).transpose(0, 2, 1, 3)
+    return cells.reshape(count, NY * PLANES, NX)
+
+
+def applied_of(mixed, cells):
     sems = pltpu.SemaphoreType.DMA((CHUNKS,))
     anywhere = pl.BlockSpec(memory_space=pl.ANY)
-    return pl.pallas_call(
+    count = cells.shape[0]
+    potential, applied = pl.pallas_call(
         apply,
         out_shape=(
-            jax.ShapeDtypeStruct(flat, jnp.float32),
-            jax.ShapeDtypeStruct(orbitals.shape, orbitals.dtype),
+            jax.ShapeDtypeStruct((NY * PLANES, NX), jnp.float32),
+            jax.ShapeDtypeStruct(cells.shape, cells.dtype),
         ),
-        in_specs=[anywhere, anywhere],
+        in_specs=[anywhere, pl.BlockSpec(memory_space=pltpu.VMEM)],
         out_specs=(anywhere, anywhere),
         scratch_shapes=[
             pltpu.VMEM((NY * PLANES, NX), jnp.float32),
-            pltpu.VMEM(flat, jnp.float32),
-            pltpu.VMEM(orbitals.shape, orbitals.dtype),
-            sems, sems, sems, sems,
+            pltpu.VMEM(cells.shape, cells.dtype),
+            sems, sems, sems,
         ],
-        compiler_params=pltpu.CompilerParams(vmem_limit_bytes=62_500_000),
-    )(mixed, orbitals)
+        compiler_params=pltpu.CompilerParams(vmem_limit_bytes=54_200_000),
+    )(mixed, cells)
+    applied = applied.reshape(count, NY, PLANES, NX).transpose(0, 2, 1, 3)
+    potential = potential.reshape(NY, PLANES, NX).transpose(1, 0, 2)
+    return potential.reshape(PLANES, NY * NX), applied.reshape(count, PLANES, NY * NX)
 
 
 def body(bands, domains, orbitals, occupations):
-    return applied_of(potential_of(orbitals, occupations, bands, domains), orbitals)
+    cells = cells_of(orbitals)
+    return applied_of(potential_of(cells, occupations, bands, domains), cells)
 
 
 def solution(mesh):

time: 54.5 us -> 53.8 us (0.987)
  Pallas kernels: 53 us -> 52.3 us
where the time goes in v5:
time: 53.8 us; the launch traced here: 52.9 us
  Pallas kernels  52.3 us (97%)
  between operations  0.65 us (1%)
    pallas_call x1, Pallas kernels, potential_of(): pl.pallas_call(functools.partial(kernel, bands, domains, 0.5 * charge_sca...  50 us
    pallas_call x1, Pallas kernels, applied_of(): pl.pallas_call(apply, out_shape=(jax.ShapeDtypeStruct((NY * PLANES, NX),...  2.29 us

profile of v5, /device:TPU:1, one launch (start us, length us, event | category | flops | bytes accessed | tf_op | source)
XLA Modules:
  0.0 52.9 jit_solution(11330711705728997083)
XLA Ops:
  0.6 0.0 copy-start
  0.6 50.0 %shard_map.77.mixed_in = f32[8192,128]{1,0:T(8,128)} custom-call(s32[8]{0:T(128)} %occupations.1, bf16[8,768,128]{2,1,0:T(8,128)(2,1)} %bitcast.15, f32[96,96]{1,0:T(8,128)} %constant.8.clone.left_in, f32[128,128]{1,0:T(8,128)} %constant.9.clone.into_in, f32[128,128]{1,0:T(8,128)} %constant.10.clone.back_in, f32[96,128]{1,0:T(8,128)} %constant.11.clone.weight_in), custom_call_target="tpu_custom_call" | custom-call | tf_op jit(solution)/shard_map/pallas_call | solution.py:699
  50.6 0.0 copy-done
  50.6 2.3 %shard_map.78 = (f32[768,128]{1,0:T(8,128)}, bf16[8,768,128]{2,1,0:T(8,128)(2,1)}) custom-call(f32[8192,128]{1,0:T(8,128)} %shard_map.77.mixed_in, bf16[8,768,128]{2,1,0:T(8,128)(2,1)S(1)} %bitcast.16), custom_call_target="tpu_custom_call" | custom-call | tf_op jit(solution)/shard_map/pallas_call | solution.py:771
Async XLA Ops:
  0.6 50.0 %copy-start = (bf16[8,4,24576]{2,1,0:T(4,128)(2,1)S(1)}, bf16[8,4,24576]{2,1,0:T(4,128)(2,1)}, u32[]{:S(2)}) copy-start(bf16[8,4,24576]{2,1,0:T(4,128)(2,1)} %param.6) | copy-start | bytes 4718596

commit v6 on v5

--- a/solution.py
+++ b/solution.py
@@ -342,10 +342,20 @@
         return 0.5 * jnp.where(even, a, e)
 
     def restrict_and_send(v, cycle):
-        g[cycle, d] = packed(v, fx, OWN, OWN + 2)
-        for i in range(1, chips):
-            tell(i, cycle).start()
-        tell(0, cycle).start()
+        for slot in (1, 2):
+            low = (slot - 1) * NY // 2
+            pairs = []
+            for at, t in ((OWN, t0), (OWN + 2, t1)):
+                for r0 in range(low, low + NY // 2, 48):
+                    t[r0:r0 + 48, :] = residual(v, fx, 0, at, r0, 48) + residual(v, fx, 0, at + 1, r0, 48)
+                n = rows1 // 2
+                pairs.append(t[pl.ds(low, n, stride=2), :] + t[pl.ds(low + 1, n, stride=2), :])
+            a = pairs[0] + pltpu.roll(pairs[0], NX - 1, 1)
+            e = pairs[1] + pltpu.roll(pairs[1], 1, 1)
+            g[cycle, d, low // 2:low // 2 + n, :] = 0.5 * jnp.where(even[:n], a, e)
+            for i in range(1, chips):
+                tell(i, slot).start()
+            tell(0, slot).start()
 
     sibling = d + 1 - 2 * lax.rem(d, 2)
     chips = domains // 2
@@ -360,7 +370,9 @@
         return remote(shares.at[d], shares.at[d], sum_s.at[2], sum_r.at[2], (dev, d))
 
     def block(cycle, origin):
-        return g.at[1, origin] if cycle else shares.at[origin]
+        if cycle == 0:
+            return shares.at[origin]
+        return g.at[1, origin, pl.ds((cycle - 1) * (rows1 // 2), rows1 // 2), :]
 
     def tell(i, cycle):
         dev = sibling if i == 0 else lax.rem(d + 2 * i, domains)
@@ -437,17 +449,39 @@
             handed(i, 0).wait_recv()
         loop(0, domains, total_share, 2)
 
+    def v_up():
+        return remote(
+            vc.at[pl.ds(OWN + 2, 2), pl.ds(PAD, NY), :], hv.at[0], hv_s.at[0], hv_r.at[0], (b, d + 1)
+        )
+
+    def v_down():
+        return remote(
+            vc.at[pl.ds(OWN, 2), pl.ds(PAD, NY), :], hv.at[1], hv_s.at[1], hv_r.at[1], (b, d - 1)
+        )
+
     def gathered_residuals():
-        for i in range(1, chips):
-            told(i, 1).wait_recv()
-            hand_on(i, 1).start()
+        for slot in (1, 2):
+            for i in range(1, chips):
+                told(i, slot).wait_recv()
+                hand_on(i, slot).start()
+
+        @pl.when(d < domains - 1)
+        def _():
+            v_up().start()
+
+        @pl.when(d > 0)
+        def _():
+            v_down().start()
+
         unpack(1, d)
         for i in range(1, chips):
             unpack(1, origin_of(i, d))
         told(0, 1).wait_recv()
+        told(0, 2).wait_recv()
         unpack(1, sibling)
         for i in range(1, chips):
             handed(i, 1).wait_recv()
+            handed(i, 2).wait_recv()
             unpack(1, origin_of(i, sibling))
 
     def unpack(cycle, origin):
@@ -585,24 +619,6 @@
     sweep(vb, fx, va, 0, *window(2))
     sweep(va, fx, vc, 0, *window(1))
     restrict_and_send(vc, 1)
-
-    def v_up():
-        return remote(
-            vc.at[pl.ds(OWN + 2, 2), pl.ds(PAD, NY), :], hv.at[0], hv_s.at[0], hv_r.at[0], (b, d + 1)
-        )
-
-    def v_down():
-        return remote(
-            vc.at[pl.ds(OWN, 2), pl.ds(PAD, NY), :], hv.at[1], hv_s.at[1], hv_r.at[1], (b, d - 1)
-        )
-
-    @pl.when(d < domains - 1)
-    def _():
-        v_up().start()
-
-    @pl.when(d > 0)
-    def _():
-        v_down().start()
 
     coarse(gathered_residuals, 1, lambda: None)
 
@@ -663,7 +679,7 @@
             for h in range(HALVES):
                 onward_copy(i, h).wait_send()
 
-    for cycle in range(2):
+    for cycle in range(3):
         for i in range(chips):
             tell(i, cycle).wait_send()
         for i in range(1, chips):
@@ -695,7 +711,7 @@
     chunk_sems = pltpu.SemaphoreType.DMA((CHUNKS,))
     near_sems = pltpu.SemaphoreType.DMA((2, CHUNKS))
     sum_sems = pltpu.SemaphoreType.DMA((3,))
-    chip_sems = pltpu.SemaphoreType.DMA((2, domains // 2))
+    chip_sems = pltpu.SemaphoreType.DMA((3, domains // 2))
     return pl.pallas_call(
         functools.partial(kernel, bands, domains, 0.5 * charge_scale / (count * bands)),
         out_shape=jax.ShapeDtypeStruct((ROOM, NX), f32),

time: 53.8 us -> 53.2 us (0.989); the launches traced: 52.9 us -> 53 us
  no operation moved by 1% of the time
where the time goes in v6:
time: 53.2 us; the launch traced here: 53 us
  Pallas kernels  52.3 us (98%)
  between operations  0.65 us (1%)
    pallas_call x1, Pallas kernels, potential_of(): pl.pallas_call(functools.partial(kernel, bands, domains, 0.5 * charge_sca...  50.1 us
    pallas_call x1, Pallas kernels, applied_of(): pl.pallas_call(apply, out_shape=(jax.ShapeDtypeStruct((NY * PLANES, NX),...  2.29 us

profile of v6, /device:TPU:1, one launch (start us, length us, event | category | flops | bytes accessed | tf_op | source)
XLA Modules:
  0.0 53.0 jit_solution(14345845006256319534)
XLA Ops:
  0.6 0.0 copy-start
  0.6 50.1 %shard_map.77.mixed_in = f32[8192,128]{1,0:T(8,128)} custom-call(s32[8]{0:T(128)} %occupations.1, bf16[8,768,128]{2,1,0:T(8,128)(2,1)} %bitcast.15, f32[96,96]{1,0:T(8,128)} %constant.8.clone.left_in, f32[128,128]{1,0:T(8,128)} %constant.9.clone.into_in, f32[128,128]{1,0:T(8,128)} %constant.10.clone.back_in, f32[96,128]{1,0:T(8,128)} %constant.11.clone.weight_in), custom_call_target="tpu_custom_call" | custom-call | tf_op jit(solution)/shard_map/pallas_call | solution.py:715
  50.7 0.0 copy-done
  50.7 2.3 %shard_map.78 = (f32[768,128]{1,0:T(8,128)}, bf16[8,768,128]{2,1,0:T(8,128)(2,1)}) custom-call(f32[8192,128]{1,0:T(8,128)} %shard_map.77.mixed_in, bf16[8,768,128]{2,1,0:T(8,128)(2,1)S(1)} %bitcast.16), custom_call_target="tpu_custom_call" | custom-call | tf_op jit(solution)/shard_map/pallas_call | solution.py:787
Async XLA Ops:
  0.6 50.1 %copy-start = (bf16[8,4,24576]{2,1,0:T(4,128)(2,1)S(1)}, bf16[8,4,24576]{2,1,0:T(4,128)(2,1)}, u32[]{:S(2)}) copy-start(bf16[8,4,24576]{2,1,0:T(4,128)(2,1)} %param.6) | copy-start | bytes 4718596

commit v7 on v6

--- a/solution.py
+++ b/solution.py
@@ -419,8 +419,9 @@
         def _():
             sum_down(outer).start()
 
-        for i in range(chips):
+        for i in range(1, chips):
             tell(i, 0).start()
+        tell(0, 0).start()
 
     order = list(range(EARLY)) + [None] + list(range(EARLY, CHUNKS))
 

time: 53.2 us -> 53.2 us (level)
  no operation moved by 1% of the time
where the time goes in v7:
time: 53.2 us; the launch traced here: 53 us
  Pallas kernels  52.3 us (98%)
  between operations  0.65 us (1%)
    pallas_call x1, Pallas kernels, potential_of(): pl.pallas_call(functools.partial(kernel, bands, domains, 0.5 * charge_sca...  50.1 us
    pallas_call x1, Pallas kernels, applied_of(): pl.pallas_call(apply, out_shape=(jax.ShapeDtypeStruct((NY * PLANES, NX),...  2.29 us

profile of v7, /device:TPU:1, one launch (start us, length us, event | category | flops | bytes accessed | tf_op | source)
XLA Modules:
  0.0 53.0 jit_solution(9786135709711844002)
XLA Ops:
  0.6 0.0 copy-start
  0.6 50.1 %shard_map.77.mixed_in = f32[8192,128]{1,0:T(8,128)} custom-call(s32[8]{0:T(128)} %occupations.1, bf16[8,768,128]{2,1,0:T(8,128)(2,1)} %bitcast.15, f32[96,96]{1,0:T(8,128)} %constant.8.clone.left_in, f32[128,128]{1,0:T(8,128)} %constant.9.clone.into_in, f32[128,128]{1,0:T(8,128)} %constant.10.clone.back_in, f32[96,128]{1,0:T(8,128)} %constant.11.clone.weight_in), custom_call_target="tpu_custom_call" | custom-call | tf_op jit(solution)/shard_map/pallas_call | solution.py:716
  50.7 0.0 copy-done
  50.7 2.3 %shard_map.78 = (f32[768,128]{1,0:T(8,128)}, bf16[8,768,128]{2,1,0:T(8,128)(2,1)}) custom-call(f32[8192,128]{1,0:T(8,128)} %shard_map.77.mixed_in, bf16[8,768,128]{2,1,0:T(8,128)(2,1)S(1)} %bitcast.16), custom_call_target="tpu_custom_call" | custom-call | tf_op jit(solution)/shard_map/pallas_call | solution.py:788
Async XLA Ops:
  0.6 50.1 %copy-start = (bf16[8,4,24576]{2,1,0:T(4,128)(2,1)S(1)}, bf16[8,4,24576]{2,1,0:T(4,128)(2,1)}, u32[]{:S(2)}) copy-start(bf16[8,4,24576]{2,1,0:T(4,128)(2,1)} %param.6) | copy-start | bytes 4718596
